TPU v7x, 32 devices: a whole 2x2x4 slice. The times are simulated.
32 devices in a mesh: dp: 8 (over y, x, core), tensor: 4 (over z).
Axes of the slice: x: 2, y: 2, z: 4, core: 2. Of those that a mesh axis runs over, the one named last changes fastest.
Arguments:
- tokens: bfloat16 [16384, 768], P(('dp', 'tensor')), may hold values from -6 to 6
- cotangent: bfloat16 [16384, 768], P(('dp', 'tensor')), may hold values from -6 to 6
- w_qkv: float32 [3, 768, 768], P(None, 'dp', 'tensor'), may hold values from -0.21875 to 0.21875
- w_out: float32 [768, 768], P('tensor', 'dp'), may hold values from -1.75 to 1.75
- w_up: float32 [768, 3072], P('dp', 'tensor'), may hold values from -0.21875 to 0.21875
- w_down: float32 [3072, 768], P('tensor', 'dp'), may hold values from -0.109375 to 0.109375
- vectors: float32 [9216], replicated, may hold values from -0.9 to 1.5, as said below
- m_qkv: float32 [3, 768, 768], P(None, 'dp', 'tensor'), may hold values from -80 to 80
- v_qkv: float32 [3, 768, 768], P(None, 'dp', 'tensor'), may hold values from 16.384 to 65.536
- m_out: float32 [768, 768], P('tensor', 'dp'), may hold values from -24 to 24
- v_out: float32 [768, 768], P('tensor', 'dp'), may hold values from 1.47456 to 5.89824
- m_up: float32 [768, 3072], P('dp', 'tensor'), may hold values from -24 to 24
- v_up: float32 [768, 3072], P('dp', 'tensor'), may hold values from 1.47456 to 5.89824
- m_down: float32 [3072, 768], P('tensor', 'dp'), may hold values from -56 to 56
- v_down: float32 [3072, 768], P('tensor', 'dp'), may hold values from 6.88128 to 27.8528
- m_vec: float32 [9216], replicated, may hold values from -80 to 80
- v_vec: float32 [9216], replicated, may hold values from 16.384 to 65.536
Outputs:
- output: bfloat16 [16384, 768], P(('dp', 'tensor'))
- grad_tokens: float32 [16384, 768], P(('dp', 'tensor'))
- qkv_mean: float32 [3, 768, 768], P(None, 'dp', 'tensor')
- qkv_square: float32 [3, 768, 768], P(None, 'dp', 'tensor')
- qkv_weight: float32 [3, 768, 768], P(None, 'dp', 'tensor')
- out_mean: float32 [768, 768], P('tensor', 'dp')
- out_square: float32 [768, 768], P('tensor', 'dp')
- out_weight: float32 [768, 768], P('tensor', 'dp')
- up_mean: float32 [768, 3072], P('dp', 'tensor')
- up_square: float32 [768, 3072], P('dp', 'tensor')
- up_weight: float32 [768, 3072], P('dp', 'tensor')
- down_mean: float32 [3072, 768], P('tensor', 'dp')
- down_square: float32 [3072, 768], P('tensor', 'dp')
- down_weight: float32 [3072, 768], P('tensor', 'dp')
- vec_mean: float32 [9216], replicated
- vec_square: float32 [9216], replicated
- vec_values: float32 [9216], replicated
Inputs may be any that keep to these rules, and one draw needn't show every extreme that they name: `vectors`: entries 0 to 767 and 1536 to 2303 are norm gains between 0.5 and 1.5; all others are shifts and biases.
All inputs are finite; a program needn't handle non-finite values.
Results may differ from a plain program's by a relative error of at most 0.017.
Values may be sent and summed in bfloat16 or wider, within the bound.
A program may use at most 128 MiB of HBM per device.

v0:
```python
import jax
import jax.numpy as jnp
from jax import lax
from jax.sharding import PartitionSpec as P

D = 768
HEAD = 64
FF = 3072
LENGTH = 1024
STEP = 10


EPSILON = 1e-05
BETA_ONE = 0.9
BETA_TWO = 0.999
ADAM_EPSILON = 1e-08
WEIGHT_DECAY = 0.1
VECTOR_RATE = 0.3
MASKED = -1e30


def layer_norm(values, gain_row, shift_row):
    row_mean = jnp.mean(values, axis=-1, keepdims=True)
    centred = values - row_mean
    spread = jnp.mean(centred * centred, axis=-1, keepdims=True)
    return centred * lax.rsqrt(spread + EPSILON) * gain_row + shift_row


def block_scores(queries, key_rows, first_row):
    score_scale = queries.shape[-1] ** (-0.5)
    scores = (
        jnp.einsum("qhd,khd->hqk", queries, key_rows, preferred_element_type=jnp.float32)
        * score_scale
    )
    query_index = first_row + jnp.arange(queries.shape[0])
    key_index = jnp.arange(key_rows.shape[0])
    causal = query_index[:, None] >= key_index[None, :]
    return jnp.where(causal[None], scores, MASKED)


def attend_forward(inputs):
    queries, key_rows, values = inputs
    length = queries.shape[0]
    block_rows = min(512, length)
    outputs = []
    totals = []
    for first_row in range(0, length, block_rows):
        scores = block_scores(queries[first_row : first_row + block_rows], key_rows, first_row)
        largest = jnp.max(scores, axis=-1, keepdims=True)
        weights = jnp.exp(scores - largest)
        exp_total = jnp.sum(weights, axis=-1, keepdims=True)
        softmax_rows = (weights / exp_total).astype(jnp.bfloat16)
        outputs.append(
            jnp.einsum("hqk,khd->qhd", softmax_rows, values, preferred_element_type=jnp.float32)
        )
        totals.append(largest + jnp.log(exp_total))
    return (jnp.concatenate(outputs, axis=0).astype(jnp.bfloat16), jnp.concatenate(totals, axis=1))


def attend_backward(inputs):
    queries, key_rows, values, log_sums, grad_out = inputs
    length = queries.shape[0]
    block_rows = min(512, length)
    score_scale = queries.shape[-1] ** (-0.5)
    grad_queries = []
    grad_keys = jnp.zeros(key_rows.shape, jnp.float32)
    grad_values = jnp.zeros(values.shape, jnp.float32)
    for first_row in range(0, length, block_rows):
        query_block = queries[first_row : first_row + block_rows]
        out_block = grad_out[first_row : first_row + block_rows]
        scores = block_scores(query_block, key_rows, first_row)
        softmax_rows = jnp.exp(scores - log_sums[:, first_row : first_row + block_rows])
        grad_probs = jnp.einsum(
            "qhd,khd->hqk", out_block, values, preferred_element_type=jnp.float32
        )
        inner_sum = jnp.sum(softmax_rows * grad_probs, axis=-1, keepdims=True)
        grad_scores = (softmax_rows * (grad_probs - inner_sum)).astype(jnp.bfloat16)
        grad_queries.append(
            jnp.einsum("hqk,khd->qhd", grad_scores, key_rows, preferred_element_type=jnp.float32)
            * score_scale
        )
        grad_keys = (
            grad_keys
            + jnp.einsum(
                "hqk,qhd->khd", grad_scores, query_block, preferred_element_type=jnp.float32
            )
            * score_scale
        )
        grad_values = grad_values + jnp.einsum(
            "hqk,qhd->khd",
            softmax_rows.astype(jnp.bfloat16),
            out_block,
            preferred_element_type=jnp.float32,
        )
    return (
        jnp.concatenate(grad_queries, axis=0).astype(jnp.bfloat16),
        grad_keys.astype(jnp.bfloat16),
        grad_values.astype(jnp.bfloat16),
    )


def adam_update(weight, gradient, first_moment, second_moment, step_rate, decay_rate):
    first_new = BETA_ONE * first_moment + (1.0 - BETA_ONE) * gradient
    second_new = BETA_TWO * second_moment + (1.0 - BETA_TWO) * gradient * gradient
    first_hat = first_new / (1.0 - BETA_ONE**STEP)
    second_hat = second_new / (1.0 - BETA_TWO**STEP)
    weight_new = weight - step_rate * (
        first_hat / (jnp.sqrt(second_hat) + ADAM_EPSILON) + decay_rate * weight
    )
    return (first_new, second_new, weight_new)


def on_device(
    tokens,
    cotangent,
    w_qkv,
    w_out,
    w_up,
    w_down,
    vectors,
    m_qkv,
    v_qkv,
    m_out,
    v_out,
    m_up,
    v_up,
    m_down,
    v_down,
    m_vec,
    v_vec,
):
    model_width = tokens.shape[1]
    local_rows = tokens.shape[0]
    head_cols = w_qkv.shape[2]
    unit_cols = w_up.shape[1]
    full_units = vectors.shape[0] - 8 * model_width
    tensor_rank = lax.axis_index("tensor")
    query_bias = lax.dynamic_slice_in_dim(
        vectors, 6 * model_width + tensor_rank * head_cols, head_cols
    )
    value_bias = lax.dynamic_slice_in_dim(
        vectors, 7 * model_width + tensor_rank * head_cols, head_cols
    )
    qkv_full, out_full, up_full, down_full = (
        lax.all_gather(w_qkv.astype(jnp.bfloat16), "dp", axis=1, tiled=True),
        lax.all_gather(w_out.astype(jnp.bfloat16), "dp", axis=1, tiled=True),
        lax.all_gather(w_up.astype(jnp.bfloat16), "dp", axis=0, tiled=True),
        lax.all_gather(w_down.astype(jnp.bfloat16), "dp", axis=1, tiled=True),
    )
    token_rows = tokens.astype(jnp.float32)
    cot_rows = cotangent.astype(jnp.float32)
    normed_one, norm_one_pull = jax.vjp(
        layer_norm, token_rows, vectors[0:model_width], vectors[model_width : 2 * model_width]
    )
    normed_one = normed_one.astype(jnp.bfloat16)
    normed_group = lax.all_gather(normed_one, "tensor", axis=0, tiled=True)
    group_rows = normed_group.shape[0]
    projected = jnp.einsum(
        "nd,cde->cne", normed_group, qkv_full, preferred_element_type=jnp.float32
    )
    biases = jnp.stack([query_bias, jnp.zeros_like(query_bias), value_bias])
    projected = (projected + biases[:, None, :]).astype(jnp.bfloat16)
    heads_local = head_cols // HEAD
    sequences = group_rows // LENGTH
    split_heads = projected.reshape(3, sequences, LENGTH, heads_local, HEAD)
    attended, log_sums = lax.map(attend_forward, (split_heads[0], split_heads[1], split_heads[2]))
    attended_rows = attended.reshape(group_rows, head_cols)
    branch = lax.psum_scatter(
        jnp.dot(
            lax.slice_in_dim(attended_rows, 0, lax.axis_size("tensor") * local_rows, axis=0),
            out_full,
            preferred_element_type=jnp.float32,
        ).astype(jnp.bfloat16),
        "tensor",
        scatter_dimension=0,
        tiled=True,
    ).astype(jnp.float32)
    hidden = token_rows + branch + vectors[4 * model_width : 5 * model_width]
    normed_two, norm_two_pull = jax.vjp(
        layer_norm,
        hidden,
        vectors[2 * model_width : 3 * model_width],
        vectors[3 * model_width : 4 * model_width],
    )
    normed_two = normed_two.astype(jnp.bfloat16)
    down_bias = vectors[5 * model_width : 6 * model_width]
    up_bias = lax.dynamic_slice_in_dim(
        vectors, 8 * model_width + tensor_rank * unit_cols, unit_cols
    )
    normed_two_group = lax.all_gather(normed_two, "tensor", axis=0, tiled=True)
    pre_act = jnp.dot(normed_two_group, up_full, preferred_element_type=jnp.float32) + up_bias
    active, gelu_pull = jax.vjp(jax.nn.gelu, pre_act)
    active = active.astype(jnp.bfloat16)
    output = (
        hidden
        + lax.psum_scatter(
            jnp.dot(
                lax.slice_in_dim(active, 0, lax.axis_size("tensor") * local_rows, axis=0),
                down_full,
                preferred_element_type=jnp.float32,
            ).astype(jnp.bfloat16),
            "tensor",
            scatter_dimension=0,
            tiled=True,
        ).astype(jnp.float32)
        + down_bias
    )
    cot_group = lax.all_gather(cotangent, "tensor", axis=0, tiled=True)
    grad_active = jnp.einsum("nd,fd->nf", cot_group, down_full, preferred_element_type=jnp.float32)
    grad_pre = gelu_pull(grad_active)[0].astype(jnp.bfloat16)
    grad_up = jnp.einsum(
        "nd,nf->df", normed_two_group, grad_pre, preferred_element_type=jnp.float32
    )
    grad_down = jnp.einsum("nf,nd->fd", active, cot_group, preferred_element_type=jnp.float32)
    grad_normed_two = lax.psum_scatter(
        jnp.einsum(
            "nf,df->nd",
            lax.slice_in_dim(grad_pre, 0, lax.axis_size("tensor") * local_rows, axis=0),
            up_full,
            preferred_element_type=jnp.float32,
        ).astype(jnp.bfloat16),
        "tensor",
        scatter_dimension=0,
        tiled=True,
    ).astype(jnp.float32)
    up_part = jnp.sum(grad_pre.astype(jnp.float32), axis=0)
    up_bias_grad = lax.dynamic_update_slice_in_dim(
        jnp.zeros((full_units,), jnp.float32), up_part, tensor_rank * unit_cols, 0
    )
    grad_from_norm, grad_gain_two, grad_shift_two = norm_two_pull(grad_normed_two)
    grad_hidden = cot_rows + grad_from_norm
    hidden_group = lax.all_gather(grad_hidden.astype(jnp.bfloat16), "tensor", axis=0, tiled=True)
    grad_attended = jnp.einsum(
        "nd,ed->ne", hidden_group, out_full, preferred_element_type=jnp.float32
    ).astype(jnp.bfloat16)
    grad_out_w = jnp.einsum(
        "ne,nd->ed", attended_rows, hidden_group, preferred_element_type=jnp.float32
    )
    grad_split = grad_attended.reshape(sequences, LENGTH, heads_local, HEAD)
    grad_query, grad_key, grad_value = lax.map(
        attend_backward, (split_heads[0], split_heads[1], split_heads[2], log_sums, grad_split)
    )
    grad_proj = jnp.stack(
        [
            grad_query.reshape(group_rows, head_cols),
            grad_key.reshape(group_rows, head_cols),
            grad_value.reshape(group_rows, head_cols),
        ]
    )
    grad_qkv_w = jnp.einsum(
        "nd,cne->cde", normed_group, grad_proj, preferred_element_type=jnp.float32
    )
    grad_normed_one = lax.psum_scatter(
        jnp.einsum(
            "cne,cde->nd",
            lax.slice_in_dim(grad_proj, 0, lax.axis_size("tensor") * local_rows, axis=1),
            qkv_full,
            preferred_element_type=jnp.float32,
        ).astype(jnp.bfloat16),
        "tensor",
        scatter_dimension=0,
        tiled=True,
    ).astype(jnp.float32)
    grad_from_first, grad_gain_one, grad_shift_one = norm_one_pull(grad_normed_one)
    grad_tokens = grad_hidden + grad_from_first
    bias_sums = jnp.sum(grad_proj.astype(jnp.float32), axis=1)
    zero_width = jnp.zeros((model_width,), jnp.float32)
    query_part = lax.dynamic_update_slice_in_dim(
        zero_width, bias_sums[0], tensor_rank * head_cols, 0
    )
    value_part = lax.dynamic_update_slice_in_dim(
        zero_width, bias_sums[2], tensor_rank * head_cols, 0
    )
    vector_part = jnp.concatenate(
        [
            grad_gain_one,
            grad_shift_one,
            grad_gain_two,
            grad_shift_two,
            jnp.sum(grad_hidden, axis=0),
            jnp.sum(cot_rows, axis=0),
            query_part,
            value_part,
            up_bias_grad,
        ]
    )
    vector_grad = lax.psum(vector_part, ("dp", "tensor"))
    grad_qkv, grad_out, grad_up_own, grad_down_own = (
        lax.psum_scatter(grad_qkv_w, "dp", scatter_dimension=1, tiled=True),
        lax.psum_scatter(grad_out_w, "dp", scatter_dimension=1, tiled=True),
        lax.psum_scatter(grad_up, "dp", scatter_dimension=0, tiled=True),
        lax.psum_scatter(grad_down, "dp", scatter_dimension=1, tiled=True),
    )
    qkv_new = adam_update(w_qkv, grad_qkv, m_qkv, v_qkv, D ** (-0.5), WEIGHT_DECAY)
    out_new = adam_update(w_out, grad_out, m_out, v_out, (D // 64) ** (-0.5), WEIGHT_DECAY)
    up_new = adam_update(w_up, grad_up_own, m_up, v_up, D ** (-0.5), WEIGHT_DECAY)
    down_new = adam_update(w_down, grad_down_own, m_down, v_down, FF ** (-0.5), WEIGHT_DECAY)
    vec_new = adam_update(vectors, vector_grad, m_vec, v_vec, VECTOR_RATE, 0.0)
    return (
        output.astype(jnp.bfloat16),
        grad_tokens,
        qkv_new[0],
        qkv_new[1],
        qkv_new[2],
        out_new[0],
        out_new[1],
        out_new[2],
        up_new[0],
        up_new[1],
        up_new[2],
        down_new[0],
        down_new[1],
        down_new[2],
        vec_new[0],
        vec_new[1],
        vec_new[2],
    )


def solution(mesh):
    return jax.shard_map(
        on_device,
        mesh=mesh,
        in_specs=(
            P(("dp", "tensor"), None),
            P(("dp", "tensor"), None),
            P(None, "dp", "tensor"),
            P("tensor", "dp"),
            P("dp", "tensor"),
            P("tensor", "dp"),
            P(),
            P(None, "dp", "tensor"),
            P(None, "dp", "tensor"),
            P("tensor", "dp"),
            P("tensor", "dp"),
            P("dp", "tensor"),
            P("dp", "tensor"),
            P("tensor", "dp"),
            P("tensor", "dp"),
            P(),
            P(),
        ),
        out_specs=(
            P(("dp", "tensor"), None),
            P(("dp", "tensor"), None),
            P(None, "dp", "tensor"),
            P(None, "dp", "tensor"),
            P(None, "dp", "tensor"),
            P("tensor", "dp"),
            P("tensor", "dp"),
            P("tensor", "dp"),
            P("dp", "tensor"),
            P("dp", "tensor"),
            P("dp", "tensor"),
            P("tensor", "dp"),
            P("tensor", "dp"),
            P("tensor", "dp"),
            P(),
            P(),
            P(),
        ),
        check_vma=False,
    )
```

profile of v0, /device:TPU:0, one launch (start us, length us, event | category | flops | bytes accessed | tf_op | source)
XLA Modules:
  0.0 834.5 jit_solution(124583361579584719)
XLA Ops:
  13.0 2.4 fusion.107
  15.7 14.6 %all_gather.25 = bf16[3,768,192]{2,0,1:T(4,128)(2,1)S(1)} all-gather(bf16[3,96,192]{2,0,1:T(4,128)(2,1)S(1)} %copy.95), channel_id=1, replica_groups=mesh['dp'=8,'tensor'=4] {'dp'}, dimensions={1}, use_global_device_ids=true | all-gather | bytes 995328 | tf_op jit(solution)/shard_map/all_gather | solution.py:145
  30.4 2.0 copy.96
  32.5 8.5 %all_gather.26 = bf16[192,768]{0,1:T(8,128)(2,1)S(1)} all-gather(bf16[192,96]{0,1:T(8,128)(2,1)S(1)} %copy.101), channel_id=1, replica_groups=mesh['dp'=8,'tensor'=4] {'dp'}, dimensions={1}, use_global_device_ids=true | all-gather | bytes 331776 | tf_op jit(solution)/shard_map/all_gather | solution.py:146
  41.9 39.8 %all-gather.7.cloned.1.call-done = bf16[2048,768]{1,0:T(8,128)(2,1)} async-done(((bf16[512,768]{1,0:T(8,128)(2,1)}), bf16[2048,768]{1,0:T(8,128)(2,1)}) %all-gather.7.cloned.1.call-update) | async-done | bytes 3145744 | tf_op jit(solution)/shard_map/all_gather | solution.py:156
  81.7 4.1 fusion.139
  90.9 23.9 %while.26 = (s32[]{:T(128)}, bf16[2,1024,3,64]{1,3,2,0:T(8,128)(2,1)S(1)}, f32[2,3,1024,1]{2,1,3,0:T(4,128)}, bf16[2,1024,3,64]{1,3,2,0:T(8,128)(2,1)S(1)}, bf16...) while((s32[]{:T(128)}, ...), condition=%wide.region_7.8_spmd, body=%wide.region_2.7_spmd.sunk | while | flops 845087232 | bytes 45431480 | solution.py:166
  94.9 2.1 fusion.201
  100.2 2.1 fusion.204
  106.6 2.1 fusion.201
  111.9 2.1 fusion.204
  116.7 2.7 convolution_convert_fusion.2
  121.2 57.3 %reduce-scatter.13.cloned.1.call-done = bf16[512,768]{1,0:T(8,128)(2,1)} async-done(((bf16[2048,768]{1,0:T(8,128)(2,1)}), bf16[512,768]{1,0:T(8,128)(2,1)}) %reduce-scatter.13.cloned.1.call-update) | async-done | bytes 786448 | tf_op jit(solution)/shard_map/reduce_scatter | solution.py:168
  182.2 2.0 add_convert_fusion.2
  187.3 60.4 %all-gather.9.cloned.1.call-done = bf16[2048,768]{1,0:T(8,128)(2,1)} async-done(((bf16[512,768]{1,0:T(8,128)(2,1)}), bf16[2048,768]{1,0:T(8,128)(2,1)}) %all-gather.9.cloned.1.call-update) | async-done | bytes 3145744 | tf_op jit(solution)/shard_map/all_gather | solution.py:190
  247.7 7.5 fusion.140
  255.2 17.4 %all-gather.13.cloned.1.call-done = bf16[768,768]{0,1:T(8,128)(2,1)} async-done(((bf16[768,96]{0,1:T(8,128)(2,1)}), bf16[768,768]{0,1:T(8,128)(2,1)}) %all-gather.13.cloned.1.call-update) | async-done | bytes 1179664 | tf_op jit(solution)/shard_map/all_gather | solution.py:148
  272.6 65.0 %all-gather.15.cloned.1.call-done = bf16[2048,768]{1,0:T(8,128)(2,1)} async-done(((bf16[512,768]{1,0:T(8,128)(2,1)}), bf16[2048,768]{1,0:T(8,128)(2,1)}) %all-gather.15.cloned.1.call-update) | async-done | bytes 3145744 | tf_op jit(solution)/shard_map/all_gather | solution.py:208
  337.6 10.9 %convert_reduce_fusion = (f32[768]{0:T(1024)}, bf16[2048,768]{1,0:T(8,128)(2,1)S(1)}, bf16[2048,768]{1,0:T(8,128)(2,1)}) fusion(f32[2048,768]{1,0:T(8,128)} %fusion.140, f32[768]{0:T(1024)} %get-tuple-element.310, bf16[2048,768]{1,0:T(8,128)(2,1)} %all-gather.15.cloned.1.call-done, bf16[768,768]{0,1:T(8,128)(2,1)} %all-gather.13.cloned.1.call-done), kind=kOutput, calls=%fused_computation.123 | convolution fusion | flops 2455239936 | bytes 16914432 | tf_op jit(solution)/shard_map/nd,fd->nf/dot_general | solution.py:209
  350.1 4.0 convolution_convert_fusion
  354.3 6.5 convolution_convert_fusion.1
  361.0 52.3 %reduce-scatter.17.cloned.1.call-done = bf16[512,768]{1,0:T(8,128)(2,1)} async-done(((bf16[2048,768]{1,0:T(8,128)(2,1)}), bf16[512,768]{1,0:T(8,128)(2,1)}) %reduce-scatter.17.cloned.1.call-update) | async-done | bytes 786448 | tf_op jit(solution)/shard_map/reduce_scatter | solution.py:215
  413.3 2.7 convert_reduce_fusion.3
  417.2 3.0 fusion.112
  420.8 54.9 %reduce-scatter.15.cloned.1.call-done = bf16[512,768]{1,0:T(8,128)(2,1)} async-done(((bf16[2048,768]{1,0:T(8,128)(2,1)}), bf16[512,768]{1,0:T(8,128)(2,1)}) %reduce-scatter.15.cloned.1.call-update) | async-done | bytes 786448 | tf_op jit(solution)/shard_map/reduce_scatter | solution.py:196
  475.7 4.4 fusion.130
  482.3 7.0 fusion.142
  489.3 7.3 fusion.141
  496.7 49.0 %all-gather.17.cloned.1.call-done = bf16[2048,768]{1,0:T(8,128)(2,1)} async-done(((bf16[512,768]{1,0:T(8,128)(2,1)}), bf16[2048,768]{1,0:T(8,128)(2,1)}) %all-gather.17.cloned.1.call-update) | async-done | bytes 3145744 | tf_op jit(solution)/shard_map/all_gather | solution.py:232
  545.7 3.1 convolution_convert_fusion.3
  554.7 66.4 %while.27 = (s32[]{:T(128)}, bf16[2,1024,3,64]{1,3,2,0:T(8,128)(2,1)}, bf16[2,1024,3,64]{1,3,2,0:T(8,128)(2,1)}, bf16[2,1024,3,64]{1,3,2,0:T(8,128)(2,1)}, bf16[...) while((s32[]{:T(128)}, ...), condition=%wide.region_18.19_spmd, body=%wide.region_15.18_spmd.sunk | while | flops 2063660544 | bytes 158072880 | solution.py:240
  557.6 1.9 fusion.222
  559.4 1.9 fusion.223
  561.3 4.3 multiply_reduce_fusion.5
  565.7 4.4 multiply_reduce_fusion.6
  570.0 7.7 multiply_convert_fusion.4
  577.7 3.0 fusion.218
  581.8 1.8 fusion.220
  584.0 1.8 fusion.221
  590.2 1.9 fusion.222
  592.1 1.9 fusion.223
  594.0 4.3 multiply_reduce_fusion.5
  598.3 4.4 multiply_reduce_fusion.6
  602.7 8.2 multiply_convert_fusion.4
  610.9 3.0 fusion.218
  614.9 1.8 fusion.220
  617.1 1.8 fusion.221
  621.1 2.0 copy.106
  627.3 4.4 convolution_bitcast_fusion
  631.9 2.8 copy.108
  634.7 2.5 stack_reshape.11
  637.3 5.1 fusion.114
  642.4 4.2 copy.117
  646.6 4.7 reshape.301
  651.4 5.4 bitcast_convert_fusion
  658.6 1.9 copy.110
  660.5 1.8 copy.111
  662.6 2.2 multiply_subtract_fusion
  664.8 2.2 multiply_subtract_fusion.1
  667.9 6.1 reduce-scatter.27.cloned.1.call-done
  676.7 40.8 %reduce-scatter.25.cloned.1.call-done = f32[96,576]{1,0:T(8,128)} async-done(((f32[768,576]{1,0:T(8,128)}), f32[96,576]{1,0:T(8,128)}) %reduce-scatter.25.cloned.1.call-update) | async-done | bytes 221200
  723.0 57.3 %reduce-scatter.19.cloned.1.call-done = bf16[512,768]{1,0:T(8,128)(2,1)} async-done(((bf16[2048,768]{1,0:T(8,128)(2,1)}), bf16[512,768]{1,0:T(8,128)(2,1)}) %reduce-scatter.19.cloned.1.call-update) | async-done | bytes 786448 | tf_op jit(solution)/shard_map/reduce_scatter | solution.py:253
  782.0 2.1 fusion.113
  784.3 40.5 %psum.7 = f32[9216]{0:T(1024)S(1)} all-reduce(f32[9216]{0:T(1024)S(1)} %constant_dynamic-update-slice_fusion.4), channel_id=1, replica_groups=mesh['dp'=8,'tensor'=4] {'dp','tensor'}, use_global_device_ids=true, to_apply=%region_34.35 | all-reduce | flops 9216 | bytes 73728 | tf_op jit(solution)/shard_map/psum | solution.py:287
  (276 shorter events, 79.7 us)
Async XLA Ops:
  8.0 7.4 copy-start.25
  8.0 7.5 copy-start.21
  8.0 73.7 %all-gather.7.cloned.1.call-start = ((), (), s32[]{:S(2)}) async-start(), calls=%async_computation.8 | async-start | bytes 3932160 | tf_op jit(solution)/shard_map/all_gather | solution.py:156
  9.5 6.0 copy-start.33
  11.0 4.4 copy-start.38
  13.0 2.5 copy-start.31
  15.4 163.1 %reduce-scatter.13.cloned.1.call-start = ((), (), s32[]{:S(2)}) async-start(), calls=%async_computation.9 | async-start | bytes 3932160 | tf_op jit(solution)/shard_map/reduce_scatter | solution.py:168
  100.1 2.2 copy-start.27
  111.9 2.2 copy-start.27
  116.7 61.8 %copy-start.1 = (bf16[512,768]{1,0:T(8,128)(2,1)S(1)}, bf16[512,768]{1,0:T(8,128)(2,1)}, u32[]{:S(2)}) copy-start(bf16[512,768]{1,0:T(8,128)(2,1)} %param.21) | copy-start | bytes 2359300
  119.4 67.9 %all-gather.11.cloned.1.call-start = ((), (), s32[]{:S(2)}) async-start(), calls=%async_computation.11 | async-start | bytes 1327104 | tf_op jit(solution)/shard_map/all_gather | solution.py:147
  121.1 126.6 %all-gather.9.cloned.1.call-start = ((), (), s32[]{:S(2)}) async-start(), calls=%async_computation.10 | async-start | bytes 3932160 | tf_op jit(solution)/shard_map/all_gather | solution.py:190
  178.5 3.7 copy-start.7
  184.2 88.4 %all-gather.13.cloned.1.call-start = ((), (), s32[]{:S(2)}) async-start(), calls=%async_computation.12 | async-start | bytes 1327104 | tf_op jit(solution)/shard_map/all_gather | solution.py:148
  185.9 151.6 %all-gather.15.cloned.1.call-start = ((), (), s32[]{:S(2)}) async-start(), calls=%async_computation.14 | async-start | bytes 3932160 | tf_op jit(solution)/shard_map/all_gather | solution.py:208
  186.7 226.6 %reduce-scatter.17.cloned.1.call-start = ((), (), s32[]{:S(2)}) async-start(), calls=%async_computation.15 | async-start | bytes 3932160 | tf_op jit(solution)/shard_map/reduce_scatter | solution.py:215
  337.6 12.6 %copy-start.49 = (bf16[768,768]{1,0:T(8,128)(2,1)S(1)}, bf16[768,768]{1,0:T(8,128)(2,1)}, u32[]{:S(2)}) copy-start(bf16[768,768]{1,0:T(8,128)(2,1)} %all-gather.11.cloned.1.call-done) | copy-start | bytes 3538948
  354.2 121.5 %reduce-scatter.15.cloned.1.call-start = ((), (), s32[]{:S(2)}) async-start(), calls=%async_computation.13 | async-start | bytes 3932160 | tf_op jit(solution)/shard_map/reduce_scatter | solution.py:196
  360.8 184.9 %all-gather.17.cloned.1.call-start = ((), (), s32[]{:S(2)}) async-start(), calls=%async_computation.16 | async-start | bytes 3932160 | tf_op jit(solution)/shard_map/all_gather | solution.py:232
  482.2 180.4 %reduce-scatter.23.cloned.1.call-start = ((), (), s32[]{:S(2)}) async-start(), calls=%async_computation.19 | async-start | bytes 2654208 | tf_op jit(solution)/shard_map/reduce_scatter | solution.py:292
  489.3 175.5 %reduce-scatter.21.cloned.1.call-start = ((), (), s32[]{:S(2)}) async-start(), calls=%async_computation.18 | async-start | bytes 2654208 | tf_op jit(solution)/shard_map/reduce_scatter | solution.py:291
  496.7 177.4 %reduce-scatter.27.cloned.1.call-start = ((), (), s32[]{:S(2)}) async-start(), calls=%async_computation.21 | async-start | bytes 884736
  548.8 5.9 copy-start.29
  554.9 10.8 %copy-start.5 = (bf16[2,1024,3,64]{1,3,2,0:T(8,128)(2,1)}, bf16[2,1024,3,64]{1,3,2,0:T(8,128)(2,1)S(1)}, u32[]{:S(2)}) copy-start(bf16[2,1024,3,64]{1,3,2,0:T(8,128)(2,1)S(1)} %get-tuple-element.499) | copy-start | bytes 2359300 | tf_op jit(solution)/shard_map/while
  554.9 10.8 %copy-start.10 = (bf16[2,1024,3,64]{1,3,2,0:T(8,128)(2,1)}, bf16[2,1024,3,64]{1,3,2,0:T(8,128)(2,1)S(1)}, u32[]{:S(2)}) copy-start(bf16[2,1024,3,64]{1,3,2,0:T(8,128)(2,1)S(1)} %get-tuple-element.498) | copy-start | bytes 2359300 | tf_op jit(solution)/shard_map/while
  557.5 1.9 copy-start.13
  561.3 4.3 copy-start.14
  581.8 2.0 copy-start
  581.8 2.2 copy-start.15
  584.0 1.8 copy-start.18
  584.0 3.6 copy-start.4
  584.0 3.6 copy-start.6
  584.0 3.6 copy-start.11
  587.6 10.8 %copy-start.5 = (bf16[2,1024,3,64]{1,3,2,0:T(8,128)(2,1)}, bf16[2,1024,3,64]{1,3,2,0:T(8,128)(2,1)S(1)}, u32[]{:S(2)}) copy-start(bf16[2,1024,3,64]{1,3,2,0:T(8,128)(2,1)S(1)} %get-tuple-element.499) | copy-start | bytes 2359300 | tf_op jit(solution)/shard_map/while
  587.6 10.8 %copy-start.10 = (bf16[2,1024,3,64]{1,3,2,0:T(8,128)(2,1)}, bf16[2,1024,3,64]{1,3,2,0:T(8,128)(2,1)S(1)}, u32[]{:S(2)}) copy-start(bf16[2,1024,3,64]{1,3,2,0:T(8,128)(2,1)S(1)} %get-tuple-element.498) | copy-start | bytes 2359300 | tf_op jit(solution)/shard_map/while
  590.2 1.9 copy-start.13
  594.0 4.3 copy-start.14
  614.9 2.0 copy-start
  614.9 2.2 copy-start.15
  617.1 3.6 copy-start.4
  617.1 3.6 copy-start.6
  617.1 3.6 copy-start.11
  621.1 3.6 copy-start.17
  631.8 85.7 %reduce-scatter.25.cloned.1.call-start = ((), (), s32[]{:S(2)}) async-start(), calls=%async_computation.20 | async-start | bytes 2211840
  651.4 128.9 %reduce-scatter.19.cloned.1.call-start = ((), (), s32[]{:S(2)}) async-start(), calls=%async_computation.17 | async-start | bytes 3932160 | tf_op jit(solution)/shard_map/reduce_scatter | solution.py:253
  656.8 5.5 copy-start.48
  656.8 5.8 copy-start.23
  656.8 8.0 copy-start.24
  662.6 12.5 %copy-start.26 = (f32[192,96]{1,0:T(8,128)S(1)}, f32[192,96]{1,0:T(8,128)}, u32[]{:S(2)}) copy-start(f32[192,96]{1,0:T(8,128)} %param.24) | copy-start | bytes 221188
  667.4 112.8 %copy-start.2 = (bf16[512,768]{1,0:T(8,128)(2,1)S(1)}, bf16[512,768]{1,0:T(8,128)(2,1)}, u32[]{:S(2)}) copy-start(bf16[512,768]{1,0:T(8,128)(2,1)} %param.21) | copy-start | bytes 2359300
  667.4 112.8 %copy-start.32 = (f32[768]{0:T(1024)S(1)}, f32[768]{0:T(1024)}, u32[]{:S(2)}) copy-start(f32[768]{0:T(1024)} %copy-done.31) | copy-start | bytes 9220
  667.4 112.8 %copy-start.34 = (f32[512]{0:T(512)S(1)}, f32[512]{0:T(512)}, u32[]{:S(2)}) copy-start(f32[512]{0:T(512)} %copy-done.33) | copy-start | bytes 6148
  718.6 63.4 %copy-start.42 = (f32[512]{0:T(512)S(1)}, f32[512]{0:T(512)}, u32[]{:S(2)}) copy-start(f32[512]{0:T(512)} %copy-done.41) | copy-start | bytes 6148
  718.7 63.4 %copy-start.39 = (f32[512]{0:T(512)S(1)}, f32[512]{0:T(512)}, u32[]{:S(2)}) copy-start(f32[512]{0:T(512)} %copy-done.38) | copy-start | bytes 6148
  718.8 65.3 %copy-start.35 = (f32[9216]{0:T(1024)S(1)}, f32[9216]{0:T(1024)}, u32[]{:S(2)}) copy-start(f32[9216]{0:T(1024)} %custom-call) | copy-start | bytes 110596
  718.8 65.3 %copy-start.45 = (f32[768]{0:T(1024)S(1)}, f32[768]{0:T(1024)}, u32[]{:S(2)}) copy-start(f32[768]{0:T(1024)} %get-tuple-element.232) | copy-start | bytes 9220
  718.9 65.3 %copy-start.44 = (f32[768]{0:T(1024)S(1)}, f32[768]{0:T(1024)}, u32[]{:S(2)}) copy-start(f32[768]{0:T(1024)} %get-tuple-element.236) | copy-start | bytes 9220
  718.9 65.3 %copy-start.47 = (f32[768]{0:T(1024)S(1)}, f32[768]{0:T(1024)}, u32[]{:S(2)}) copy-start(f32[768]{0:T(1024)} %get-tuple-element.275) | copy-start | bytes 9220
  718.9 65.3 %copy-start.46 = (f32[768]{0:T(1024)S(1)}, f32[768]{0:T(1024)}, u32[]{:S(2)}) copy-start(f32[768]{0:T(1024)} %get-tuple-element.308) | copy-start | bytes 9220
  718.9 105.9 %copy-start.30 = (f32[9216]{0:T(1024)S(1)}, f32[9216]{0:T(1024)}, u32[]{:S(2)}) copy-start(f32[9216]{0:T(1024)} %param.27) | copy-start | bytes 110596
  718.9 105.9 %copy-start.36 = (f32[9216]{0:T(1024)S(1)}, f32[9216]{0:T(1024)}, u32[]{:S(2)}) copy-start(f32[9216]{0:T(1024)} %param.37) | copy-start | bytes 110596
  718.9 105.9 %copy-start.37 = (f32[9216]{0:T(1024)S(1)}, f32[9216]{0:T(1024)}, u32[]{:S(2)}) copy-start(f32[9216]{0:T(1024)} %param.36) | copy-start | bytes 110596
  720.3 105.2 %copy-start.9 = (f32[512,768]{1,0:T(8,128)S(1)}, f32[512,768]{1,0:T(8,128)}, u32[]{:S(2)}) copy-start(f32[512,768]{1,0:T(8,128)} %copy-done.8) | copy-start | bytes 4718596
  780.2 45.3 %copy-start.12 = (bf16[512,768]{1,0:T(8,128)(2,1)S(1)}, bf16[512,768]{1,0:T(8,128)(2,1)}, u32[]{:S(2)}) copy-start(bf16[512,768]{1,0:T(8,128)(2,1)} %reduce-scatter.19.cloned.1.call-done) | copy-start | bytes 2359300
  (16 other events, 16.2 us)
Sparse Core Ops, SparseCore 0:
  15.5 66.1 all-gather.6
  119.5 58.8 reduce-scatter.12
  354.3 58.8 reduce-scatter.16
  415.4 60.2 reduce-scatter.14
Sparse Core Ops, SparseCore 1:
  122.3 22.5 all-gather.10
  184.3 63.3 all-gather.8
  250.0 22.5 all-gather.12
  274.2 63.3 all-gather.14
  482.3 63.3 all-gather.16
  549.1 41.0 reduce-scatter.22
  593.7 42.3 reduce-scatter.20
  639.1 34.9 reduce-scatter.26
  677.3 40.1 reduce-scatter.24
  719.9 60.2 reduce-scatter.18
where the time goes:
time: 842 us; the launch traced here: 835 us
  waiting for transfers between devices  501 us (60%)
  matrix products  126 us (15%)
  other arithmetic  65.5 us (8%)
  blocking collectives  63.7 us (8%)
  local copies, waits for them, and re-layouts  58.9 us (7%)
  between operations  16.2 us (2%)
    all_gather x1, waiting for transfers between devices, on_device(): cot_group = lax.all_gather(cotangent, 'tensor', axis=0, tiled=True)  65 us
    all_gather x1, waiting for transfers between devices, on_device(): normed_two_group = lax.all_gather(normed_two, 'tensor', axis=0, tiled=True)  60.4 us
    reduce_scatter x1, waiting for transfers between devices, on_device(): lax.psum_scatter(jnp.dot(lax.slice_in_dim(attended_rows, 0, lax.axis_size...  57.3 us
    reduce_scatter x1, waiting for transfers between devices, on_device(): lax.psum_scatter(jnp.einsum('cne,cde->nd', lax.slice_in_dim(grad_proj, 0,...  57.3 us
    reduce_scatter x1, waiting for transfers between devices, on_device(): lax.psum_scatter(jnp.dot(lax.slice_in_dim(active, 0, lax.axis_size('tenso...  54.9 us
    reduce_scatter x1, waiting for transfers between devices, on_device(): lax.psum_scatter(jnp.einsum('nf,df->nd', lax.slice_in_dim(grad_pre, 0, la...  52.3 us
    all_gather x1, waiting for transfers between devices, on_device(): lax.all_gather(grad_hidden.astype(jnp.bfloat16), 'tensor', axis=0, tiled=...  49 us
    unnamed x16, waiting for transfers between devices  47.8 us
  transfers between devices with their start and end apart: 14, of which 11 were waited for; matrix products, arithmetic and copies ran while one was open for 20% of the time, Pallas kernels for 0%

commit v1 on v0

v1 whole, which is shorter than its diff:
```python
import jax
import jax.numpy as jnp
from jax import lax
from jax.experimental import pallas as pl
from jax.experimental.pallas import tpu as pltpu
from jax.sharding import PartitionSpec as P

D = 768
HEAD = 64
FF = 3072
LENGTH = 1024
STEP = 10


EPSILON = 1e-05
BETA_ONE = 0.9
BETA_TWO = 0.999
ADAM_EPSILON = 1e-08
WEIGHT_DECAY = 0.1
VECTOR_RATE = 0.3
MASKED = -1e30


def layer_norm(values, gain_row, shift_row):
    row_mean = jnp.mean(values, axis=-1, keepdims=True)
    centred = values - row_mean
    spread = jnp.mean(centred * centred, axis=-1, keepdims=True)
    return centred * lax.rsqrt(spread + EPSILON) * gain_row + shift_row


def adam_update(weight, gradient, first_moment, second_moment, step_rate, decay_rate):
    first_new = BETA_ONE * first_moment + (1.0 - BETA_ONE) * gradient
    second_new = BETA_TWO * second_moment + (1.0 - BETA_TWO) * gradient * gradient
    first_hat = first_new / (1.0 - BETA_ONE**STEP)
    second_hat = second_new / (1.0 - BETA_TWO**STEP)
    weight_new = weight - step_rate * (
        first_hat / (jnp.sqrt(second_hat) + ADAM_EPSILON) + decay_rate * weight
    )
    return (first_new, second_new, weight_new)


F32 = jnp.float32
BF16 = jnp.bfloat16
BLOCK = 256


def contract(left, right, left_dim, right_dim):
    return lax.dot_general(
        left, right, (((left_dim,), (right_dim,)), ((), ())), preferred_element_type=F32
    )


def block_mask(scores, first_query):
    keys = lax.broadcasted_iota(jnp.int32, scores.shape, 0)
    queries = first_query + lax.broadcasted_iota(jnp.int32, scores.shape, 1)
    return jnp.where(keys <= queries, scores, MASKED)


def forward_kernel(qkv_ref, out_ref, lse_ref):
    length = qkv_ref.shape[-1]
    scale = HEAD ** (-0.5)
    for first in range(0, length, BLOCK):
        count = first + BLOCK
        rows = slice(first, count)
        scores = contract(qkv_ref[0, 1, 0, :, :count], qkv_ref[0, 0, 0, :, rows], 0, 0) * scale
        scores = block_mask(scores, first)
        largest = jnp.max(scores, axis=0, keepdims=True)
        weights = jnp.exp(scores - largest)
        total = jnp.sum(weights, axis=0, keepdims=True)
        probs = (weights * (1.0 / total)).astype(BF16)
        out_ref[0, 0, :, rows] = contract(qkv_ref[0, 2, 0, :, :count], probs, 1, 0).astype(BF16)
        lse_ref[0, 0, :, rows] = largest + jnp.log(total)


def backward_kernel(qkv_ref, lse_ref, grad_ref, out_ref, key_sum, value_sum):
    length = qkv_ref.shape[-1]
    scale = HEAD ** (-0.5)
    key_sum[...] = jnp.zeros_like(key_sum)
    value_sum[...] = jnp.zeros_like(value_sum)
    for first in range(0, length, BLOCK):
        count = first + BLOCK
        rows = slice(first, count)
        queries = qkv_ref[0, 0, 0, :, rows]
        keys = qkv_ref[0, 1, 0, :, :count]
        grad_out = grad_ref[0, 0, :, rows]
        scores = block_mask(contract(keys, queries, 0, 0) * scale, first)
        probs = jnp.exp(scores - lse_ref[0, 0, :, rows])
        grad_probs = contract(qkv_ref[0, 2, 0, :, :count], grad_out, 0, 0)
        inner = jnp.sum(probs * grad_probs, axis=0, keepdims=True)
        grad_scores = (probs * (grad_probs - inner)).astype(BF16)
        out_ref[0, 0, 0, :, rows] = (contract(keys, grad_scores, 1, 0) * scale).astype(BF16)
        key_sum[:, :count] += contract(queries, grad_scores, 1, 1)
        value_sum[:, :count] += contract(grad_out, probs.astype(BF16), 1, 1)
    out_ref[0, 1, 0] = (key_sum[...] * scale).astype(BF16)
    out_ref[0, 2, 0] = value_sum[...].astype(BF16)


def attend_forward(qkv):
    groups, _, heads, width, length = qkv.shape
    return pl.pallas_call(
        forward_kernel,
        grid=(groups, heads),
        in_specs=[pl.BlockSpec((1, 3, 1, width, length), lambda g, h: (g, 0, h, 0, 0))],
        out_specs=[
            pl.BlockSpec((1, 1, width, length), lambda g, h: (g, h, 0, 0)),
            pl.BlockSpec((1, 1, 1, length), lambda g, h: (g, h, 0, 0)),
        ],
        out_shape=[
            jax.ShapeDtypeStruct((groups, heads, width, length), BF16),
            jax.ShapeDtypeStruct((groups, heads, 1, length), F32),
        ],
        compiler_params=pltpu.CompilerParams(vmem_limit_bytes=32 * 1024 * 1024),
        cost_estimate=pl.CostEstimate(
            flops=4 * groups * heads * length * length * width,
            bytes_accessed=8 * groups * heads * length * width,
            transcendentals=groups * heads * length * length,
        ),
    )(qkv)


def attend_backward(qkv, log_sums, grad_out):
    groups, _, heads, width, length = qkv.shape
    return pl.pallas_call(
        backward_kernel,
        grid=(groups, heads),
        in_specs=[
            pl.BlockSpec((1, 3, 1, width, length), lambda g, h: (g, 0, h, 0, 0)),
            pl.BlockSpec((1, 1, 1, length), lambda g, h: (g, h, 0, 0)),
            pl.BlockSpec((1, 1, width, length), lambda g, h: (g, h, 0, 0)),
        ],
        out_specs=pl.BlockSpec((1, 3, 1, width, length), lambda g, h: (g, 0, h, 0, 0)),
        out_shape=jax.ShapeDtypeStruct(qkv.shape, BF16),
        scratch_shapes=[pltpu.VMEM((width, length), F32), pltpu.VMEM((width, length), F32)],
        compiler_params=pltpu.CompilerParams(vmem_limit_bytes=32 * 1024 * 1024),
        cost_estimate=pl.CostEstimate(
            flops=10 * groups * heads * length * length * width,
            bytes_accessed=14 * groups * heads * length * width,
            transcendentals=groups * heads * length * length,
        ),
    )(qkv, log_sums, grad_out)


def swap(values, axis_name, distance):
    size = lax.axis_size(axis_name)
    return lax.ppermute(values, axis_name, [(i, i ^ distance) for i in range(size)])


def bit_of(axis_name, bit):
    return lax.rem(lax.axis_index(axis_name) // (1 << bit), 2)


def gather_data(values, order):
    bits = len(order)
    blocks, rows, columns = values.shape
    values = values.reshape((blocks,) + (1,) * bits + (rows, columns))
    for bit in order:
        other = swap(values, "dp", 1 << bit)
        low = bit_of("dp", bit) == 0
        values = jnp.concatenate(
            [jnp.where(low, values, other), jnp.where(low, other, values)], axis=bits - bit
        )
    return values.reshape(blocks, rows << bits, columns)


def scatter_data(values, order):
    bits = len(order)
    blocks, rows, columns = values.shape
    values = values.reshape((blocks,) + (2,) * bits + (rows >> bits, columns))
    for bit in order:
        mine = bit_of("dp", bit)
        axis = bits - bit
        other = swap(
            lax.dynamic_index_in_dim(values, 1 - mine, axis, keepdims=True), "dp", 1 << bit
        )
        kept = lax.dynamic_index_in_dim(values, mine, axis, keepdims=True)
        values = (kept.astype(F32) + other.astype(F32)).astype(BF16)
    return values.reshape(blocks, rows >> bits, columns)


def gather_blocks(shard, distances):
    return jnp.stack([shard if d == 0 else swap(shard, "tensor", d) for d in distances])


def scatter_blocks(values, distances):
    total = values[0].astype(F32)
    for index, distance in enumerate(distances):
        if distance:
            total = total + swap(values[index], "tensor", distance).astype(F32)
    return total


def reduce_all(values):
    for axis_name in ("dp", "tensor"):
        distance = 1
        while distance < lax.axis_size(axis_name):
            values = values + swap(values, axis_name, distance)
            distance *= 2
    return values


def on_device(
    tokens,
    cotangent,
    w_qkv,
    w_out,
    w_up,
    w_down,
    vectors,
    m_qkv,
    v_qkv,
    m_out,
    v_out,
    m_up,
    v_up,
    m_down,
    v_down,
    m_vec,
    v_vec,
):
    width = tokens.shape[1]
    rows = tokens.shape[0]
    head_cols = w_qkv.shape[2]
    unit_cols = w_up.shape[1]
    own_rows = w_up.shape[0]
    n_tensor = lax.axis_size("tensor")
    bits = lax.axis_size("dp").bit_length() - 1
    outer = list(range(1, bits))
    gather_one, gather_two = outer + [0], outer[::-1] + [0]
    scatter_one, scatter_two = [0] + outer, [0] + outer[::-1]
    rank = lax.axis_index("tensor")
    every = list(range(n_tensor))
    owned = every[::2]

    def vector(index):
        return vectors[index * width : (index + 1) * width]

    def ranked(first, count, distances):
        return jnp.stack(
            [
                lax.dynamic_slice_in_dim(vectors, first + (rank ^ d) * count, count)
                for d in distances
            ]
        )

    token_rows = tokens.astype(F32)
    cot_rows = cotangent.astype(F32)
    normed_one, norm_one_pull = jax.vjp(layer_norm, token_rows, vector(0), vector(1))
    normed_one = normed_one.astype(BF16)
    normed_other = swap(normed_one, "tensor", 1)
    half = lax.rem(rank, 2)
    first_half = half == 0
    normed_pair = jnp.concatenate(
        [
            jnp.where(first_half, normed_one, normed_other),
            jnp.where(first_half, normed_other, normed_one),
        ]
    )

    def exchange(values, axis):
        kept = lax.dynamic_slice_in_dim(values, half * rows, rows, axis)
        given = lax.dynamic_slice_in_dim(values, (1 - half) * rows, rows, axis)
        return kept, swap(given, "tensor", 1)

    qkv_shard = w_qkv.astype(BF16).transpose(1, 0, 2).reshape(own_rows, 3 * head_cols)
    qkv_full = gather_data(gather_blocks(qkv_shard, owned), gather_one)
    out_full = gather_data(gather_blocks(w_out.astype(BF16).T, every), gather_two)
    up_full = gather_data(gather_blocks(w_up.astype(BF16), every), gather_one)
    down_full = gather_data(gather_blocks(w_down.astype(BF16).T, every), gather_two)

    query_bias = ranked(6 * width, head_cols, owned)
    value_bias = ranked(7 * width, head_cols, owned)
    biases = jnp.concatenate([query_bias, jnp.zeros_like(query_bias), value_bias], axis=1)
    projected = jnp.einsum("jde,nd->jen", qkv_full, normed_pair, preferred_element_type=F32)
    projected = (projected + biases[:, :, None]).astype(BF16)
    heads = head_cols // HEAD
    split = projected.reshape(len(owned), 3, heads, HEAD, 2 * rows)
    attended, log_sums = attend_forward(split)
    attended = attended.reshape(len(owned), head_cols, 2 * rows)
    attended_own, attended_got = exchange(attended, 2)
    attended_all = jnp.stack([attended_own, attended_got], axis=1).reshape(
        n_tensor, head_cols, rows
    )
    branch = jnp.einsum("jen,jde->nd", attended_all, out_full, preferred_element_type=F32)
    hidden = token_rows + branch + vector(4)
    normed_two, norm_two_pull = jax.vjp(layer_norm, hidden, vector(2), vector(3))
    normed_two = normed_two.astype(BF16)
    up_bias = ranked(8 * width, unit_cols, every)
    pre_act = (
        jnp.einsum("nd,jdf->jnf", normed_two, up_full, preferred_element_type=F32)
        + up_bias[:, None, :]
    )
    active, gelu_pull = jax.vjp(jax.nn.gelu, pre_act)
    active = active.astype(BF16)
    output = (
        hidden
        + jnp.einsum("jnf,jdf->nd", active, down_full, preferred_element_type=F32)
        + vector(5)
    )
    grad_active = jnp.einsum("nd,jdf->jnf", cotangent, down_full, preferred_element_type=F32)
    grad_pre = gelu_pull(grad_active)[0].astype(BF16)
    grad_down = jnp.einsum(
        "nd,jnf->jdf", cotangent, active, preferred_element_type=F32
    ).astype(BF16)
    grad_up = jnp.einsum("nd,jnf->jdf", normed_two, grad_pre, preferred_element_type=F32).astype(
        BF16
    )
    grad_normed_two = jnp.einsum("jnf,jdf->nd", grad_pre, up_full, preferred_element_type=F32)
    up_sums = jnp.sum(grad_pre.astype(F32), axis=1)
    grad_from_norm, grad_gain_two, grad_shift_two = norm_two_pull(grad_normed_two)
    grad_hidden = cot_rows + grad_from_norm
    grad_low = grad_hidden.astype(BF16)
    grad_attended = jnp.einsum(
        "nd,jde->jen", grad_low, out_full, preferred_element_type=F32
    ).astype(BF16)
    grad_pairs = grad_attended.reshape(len(owned), 2, head_cols, rows)
    grad_other = swap(grad_pairs[:, 1], "tensor", 1)
    grad_own = grad_pairs[:, 0]
    grad_heads = jnp.concatenate(
        [
            jnp.where(first_half, grad_own, grad_other),
            jnp.where(first_half, grad_other, grad_own),
        ],
        axis=2,
    )
    grad_out_w = jnp.einsum(
        "nd,jen->jde", grad_low, attended_all, preferred_element_type=F32
    ).astype(BF16)
    grad_down_own = scatter_blocks(scatter_data(grad_down, scatter_one), every)
    grad_up_own = scatter_blocks(scatter_data(grad_up, scatter_two), every)
    grad_out_own = scatter_blocks(scatter_data(grad_out_w, scatter_one), every)
    grad_split = attend_backward(
        split, log_sums, grad_heads.reshape(len(owned), heads, HEAD, 2 * rows)
    )
    grad_proj = grad_split.reshape(len(owned), 3 * head_cols, 2 * rows)
    grad_normed_pair = jnp.einsum(
        "jen,jde->nd", grad_proj, qkv_full, preferred_element_type=F32
    ).astype(BF16)
    kept, given = exchange(grad_normed_pair, 0)
    grad_normed_one = kept.astype(F32) + given.astype(F32)
    grad_qkv_w = jnp.einsum(
        "nd,jen->jde", normed_pair, grad_proj, preferred_element_type=F32
    ).astype(BF16)
    grad_qkv_own = scatter_blocks(scatter_data(grad_qkv_w, scatter_two), owned)
    grad_from_first, grad_gain_one, grad_shift_one = norm_one_pull(grad_normed_one)
    grad_tokens = grad_hidden + grad_from_first

    def placed(parts, count, full, distances):
        result = jnp.zeros((full,), F32)
        for index, distance in enumerate(distances):
            result = lax.dynamic_update_slice_in_dim(
                result, parts[index], (rank ^ distance) * count, 0
            )
        return result

    proj_sums = jnp.sum(grad_proj.astype(F32), axis=2)
    early = reduce_all(
        jnp.concatenate(
            [
                grad_gain_two,
                grad_shift_two,
                jnp.sum(grad_hidden, axis=0),
                jnp.sum(cot_rows, axis=0),
                placed(up_sums, unit_cols, n_tensor * unit_cols, every),
            ]
        )
    )
    late = reduce_all(
        jnp.concatenate(
            [
                grad_gain_one,
                grad_shift_one,
                placed(proj_sums[:, :head_cols], head_cols, width, owned),
                placed(proj_sums[:, 2 * head_cols :], head_cols, width, owned),
            ]
        )
    )
    vector_grad = jnp.concatenate(
        [
            late[: 2 * width],
            early[: 4 * width],
            late[2 * width :],
            early[4 * width :],
        ]
    )
    grad_qkv = grad_qkv_own.reshape(own_rows, 3, head_cols).transpose(1, 0, 2)
    qkv_new = adam_update(w_qkv, grad_qkv, m_qkv, v_qkv, D ** (-0.5), WEIGHT_DECAY)
    out_new = adam_update(w_out, grad_out_own.T, m_out, v_out, (D // 64) ** (-0.5), WEIGHT_DECAY)
    up_new = adam_update(w_up, grad_up_own, m_up, v_up, D ** (-0.5), WEIGHT_DECAY)
    down_new = adam_update(w_down, grad_down_own.T, m_down, v_down, FF ** (-0.5), WEIGHT_DECAY)
    vec_new = adam_update(vectors, vector_grad, m_vec, v_vec, VECTOR_RATE, 0.0)
    return (output.astype(BF16), grad_tokens, *qkv_new, *out_new, *up_new, *down_new, *vec_new)


def solution(mesh):
    return jax.shard_map(
        on_device,
        mesh=mesh,
        in_specs=(
            P(("dp", "tensor"), None),
            P(("dp", "tensor"), None),
            P(None, "dp", "tensor"),
            P("tensor", "dp"),
            P("dp", "tensor"),
            P("tensor", "dp"),
            P(),
            P(None, "dp", "tensor"),
            P(None, "dp", "tensor"),
            P("tensor", "dp"),
            P("tensor", "dp"),
            P("dp", "tensor"),
            P("dp", "tensor"),
            P("tensor", "dp"),
            P("tensor", "dp"),
            P(),
            P(),
        ),
        out_specs=(
            P(("dp", "tensor"), None),
            P(("dp", "tensor"), None),
            P(None, "dp", "tensor"),
            P(None, "dp", "tensor"),
            P(None, "dp", "tensor"),
            P("tensor", "dp"),
            P("tensor", "dp"),
            P("tensor", "dp"),
            P("dp", "tensor"),
            P("dp", "tensor"),
            P("dp", "tensor"),
            P("tensor", "dp"),
            P("tensor", "dp"),
            P("tensor", "dp"),
            P(),
            P(),
            P(),
        ),
        check_vma=False,
    )
```

time: 842 us -> 453 us (0.54)
  waiting for transfers between devices: 501 us -> 192 us
  matrix products: 126 us -> 41.8 us
  blocking collectives: 63.7 us -> 0 us
  starting transfers between devices: 1.3 us -> 62.6 us
  Pallas kernels: 0 us -> 30.6 us
  other arithmetic: 65.5 us -> 50.5 us
  between operations: 16.2 us -> 2.65 us
    all_gather x6 -> x0, waiting for transfers between devices: 232 us -> none  [the longest x1 65 us: on_device(): cot_group = lax.all_gather(cotangent, 'tensor', axis=0, tiled=True)]
    reduce_scatter x6 -> x0, waiting for transfers between devices: 222 us -> none  [the longest x1 57.3 us: on_device(): lax.psum_scatter(jnp.dot(lax.slice_in_dim(attended_rows, 0, lax.axis_size...]
    ppermute x0 -> x58, waiting for transfers between devices: none -> 192 us  [swap(): lax.ppermute(values, axis_name, [(i, i ^ distance) for i in range(size)])]
    dot_general x38 -> x12, matrix products: 118 us -> 41.8 us  [the longest x1 9.07 us: on_device(): jnp.einsum('jnf,jdf->nd', active, down_full, preferred_element_type=F32)]
    ppermute x0 -> x58, starting transfers between devices: none -> 62.6 us  [swap(): lax.ppermute(values, axis_name, [(i, i ^ distance) for i in range(size)])]
    unnamed x16 -> x0, waiting for transfers between devices: 47.8 us -> none
    psum x1 -> x0, blocking collectives: 40.5 us -> none  [on_device(): vector_grad = lax.psum(vector_part, ('dp', 'tensor'))]
    pallas_call x0 -> x2, Pallas kernels: none -> 30.6 us  [the longest x1 16.5 us: attend_backward(): pl.pallas_call(backward_kernel, grid=(groups, heads), in_specs=[pl.BlockS...]
  transfers between devices with their start and end apart: 14 -> 58, of which waited for: 11 -> 30; matrix products, arithmetic and copies ran while one was open for 20% -> 22% of each run, Pallas kernels for 0% -> 7%
where the time goes in v1:
time: 453 us; the launch traced here: 446 us
  waiting for transfers between devices  192 us (42%)
  local copies, waits for them, and re-layouts  65.9 us (15%)
  starting transfers between devices  62.6 us (14%)
  other arithmetic  50.5 us (11%)
  matrix products  41.8 us (9%)
  Pallas kernels  30.6 us (7%)
    ppermute x58, waiting for transfers between devices, swap(): lax.ppermute(values, axis_name, [(i, i ^ distance) for i in range(size)])  192 us
    ppermute x58, starting transfers between devices, swap(): lax.ppermute(values, axis_name, [(i, i ^ distance) for i in range(size)])  62.6 us
    unnamed x165, local copies, waits for them, and re-layouts  21.9 us
    pallas_call x1, Pallas kernels, attend_backward(): pl.pallas_call(backward_kernel, grid=(groups, heads), in_specs=[pl.BlockS...  16.5 us
    pallas_call x1, Pallas kernels, attend_forward(): pl.pallas_call(forward_kernel, grid=(groups, heads), in_specs=[pl.BlockSp...  14.2 us
    convert_element_type x12, other arithmetic, scatter_data(): values = (kept.astype(F32) + other.astype(F32)).astype(BF16)  14.1 us
    dot_general x1, matrix products, on_device(): jnp.einsum('jnf,jdf->nd', active, down_full, preferred_element_type=F32)  9.07 us
  transfers between devices with their start and end apart: 58, of which 30 were waited for; matrix products, arithmetic and copies ran while one was open for 22% of the time, Pallas kernels for 7%

profile of v1, /device:TPU:0, one launch (start us, length us, event | category | flops | bytes accessed | tf_op | source)
XLA Modules:
  0.0 446.0 jit_solution(10565227132772873032)
XLA Ops:
  1.7 5.1 %collective-permute-start.8 = (bf16[96,192]{0,1:T(8,128)(2,1)S(1)}, bf16[96,192]{0,1:T(8,128)(2,1)S(1)}, u32[]{:S(2)}, u32[]{:S(2)}) collective-permute-start(bf16[96,192]{0,1:T(8,128)(2,1)S(1)} %get-tuple-element.112), channel_id=1, source_target_pairs={{0,3},{1,2},{2,1},{3,0},{4,7},{5,6},{6,5},{7,4},{8,11},{9,10},{10,... | collective-permute-start | bytes 110600 | tf_op jit(solution)/shard_map/ppermute | solution.py:145
  9.1 3.7 collective-permute-start.14
  19.7 2.4 collective-permute-start
  22.1 1.9 collective-permute-start.4
  24.8 5.5 %collective-permute-done = bf16[96,576]{0,1:T(8,128)(2,1)S(1)} collective-permute-done((bf16[96,576]{0,1:T(8,128)(2,1)S(1)}, bf16[96,576]{0,1:T(8,128)(2,1)S(1)}, u32[]{:S(2)}, u32[]{:S(2)}) %collective-permute-start) | collective-permute-done | bytes 110624 | tf_op jit(solution)/shard_map/ppermute | solution.py:145
  34.4 1.9 collective-permute-done.9
  37.4 3.7 collective-permute-done.1
  43.5 10.3 %collective-permute-done.15 = bf16[4,1,1,1,96,768]{5,4,0,3,2,1:T(8,128)(2,1)S(1)} collective-permute-done((bf16[4,1,1,1,96,768]{5,4,0,3,2,1:T(8,128)(2,1)S(1)}, bf16[4,1,1,1,96,768]{5,4,0,3,2,1:T(8,128)(2,1)S(1)}, u32[]{:S(2)}, u32[]{:S(2)}) %collective-permute-start.15) | collective-permute-done | bytes 589856 | tf_op jit(solution)/shard_map/ppermute | solution.py:145
  55.1 3.6 collective-permute-done.10
  59.9 15.5 %collective-permute-done.16 = bf16[4,1,2,1,96,768]{5,4,0,3,2,1:T(8,128)(2,1)S(1)} collective-permute-done((bf16[4,1,2,1,96,768]{5,4,0,3,2,1:T(8,128)(2,1)S(1)}, bf16[4,1,2,1,96,768]{5,4,0,3,2,1:T(8,128)(2,1)S(1)}, u32[]{:S(2)}, u32[]{:S(2)}) %collective-permute-start.16) | collective-permute-done | bytes 1179680 | tf_op jit(solution)/shard_map/ppermute | solution.py:145
  77.7 2.4 add_convert_fusion.2
  80.2 14.2 %shard_map.296 = (bf16[2,3,64,1024]{3,2,1,0:T(8,128)(2,1)S(1)}, f32[2,3,1,1024]{3,2,1,0:T(1,128)S(1)}) custom-call(bf16[2,3,3,64,1024]{4,3,2,1,0:T(8,128)(2,1)S(1)} %bitcast.260), custom_call_target="tpu_custom_call" | custom-call | flops 1610612736 | bytes 3145728 | tf_op jit(solution)/shard_map/pallas_call | solution.py:100
  95.3 1.9 collective-permute-start.5
  97.8 2.8 copy.51
  100.6 5.7 %reshape.210 = bf16[4,768,192]{1,2,0:T(8,128)(2,1)} reshape(bf16[4,2,2,2,96,192]{4,3,2,1,5,0:T(2,128)(2,1)} %copy.51) | data formatting | bytes 2359296 | tf_op jit(solution)/shard_map/reshape | solution.py:162
  110.1 2.2 broadcast_select_fusion.3
  113.2 2.1 copy-done.14
  115.3 2.7 fusion.53
  118.1 3.8 convolution_convert_fusion
  122.1 2.0 copy-done.12
  124.1 4.7 %collective-permute-done.42 = bf16[4,2,2,1,96,768]{5,4,3,2,1,0:T(8,128)(2,1)} collective-permute-done((bf16[4,2,2,1,96,768]{5,4,3,2,1,0:T(8,128)(2,1)S(1)}, bf16[4,2,2,1,96,768]{5,4,3,2,1,0:T(8,128)(2,1)}, u32[]{:S(2)}, u32[]{:S(2)}) %collective-permute-start.42) | collective-permute-done | bytes 2359328 | tf_op jit(solution)/shard_map/ppermute | solution.py:145
  128.8 3.1 add_convert_fusion
  134.5 26.8 %collective-permute-done.43 = bf16[4,2,1,1,96,768]{5,4,3,2,1,0:T(8,128)(2,1)} collective-permute-done((bf16[4,2,1,1,96,768]{5,4,3,2,1,0:T(8,128)(2,1)}, bf16[4,2,1,1,96,768]{5,4,3,2,1,0:T(8,128)(2,1)}, u32[]{:S(2)}, u32[]{:S(2)}) %collective-permute-start.43) | collective-permute-done | bytes 1179680 | tf_op jit(solution)/shard_map/ppermute | solution.py:145
  164.5 14.0 %collective-permute-done.44 = bf16[4,1,1,1,96,768]{5,4,3,2,1,0:T(8,128)(2,1)S(1)} collective-permute-done((bf16[4,1,1,1,96,768]{5,4,3,2,1,0:T(8,128)(2,1)S(1)}, bf16[4,1,1,1,96,768]{5,4,3,2,1,0:T(8,128)(2,1)S(1)}, u32[]{:S(2)}, u32[]{:S(2)}) %collective-permute-start.44) | collective-permute-done | bytes 589856 | tf_op jit(solution)/shard_map/ppermute | solution.py:145
  179.8 3.1 collective-permute-start.47
  184.3 4.2 collective-permute-done.47
  188.5 6.2 %collective-permute-done.46 = bf16[96,768]{1,0:T(8,128)(2,1)S(1)} collective-permute-done((bf16[96,768]{1,0:T(8,128)(2,1)S(1)}, bf16[96,768]{1,0:T(8,128)(2,1)S(1)}, u32[]{:S(2)}, u32[]{:S(2)}) %collective-permute-start.46) | collective-permute-done | bytes 147488 | tf_op jit(solution)/shard_map/ppermute | solution.py:145
  197.5 2.7 collective-permute-start.18
  200.2 4.2 collective-permute-done.20
  204.4 4.3 collective-permute-done.19
  209.7 14.0 %collective-permute-done.21 = bf16[4,1,1,1,96,768]{5,4,0,3,2,1:T(8,128)(2,1)S(1)} collective-permute-done((bf16[4,1,1,1,96,768]{5,4,0,3,2,1:T(8,128)(2,1)S(1)}, bf16[4,1,1,1,96,768]{5,4,0,3,2,1:T(8,128)(2,1)S(1)}, u32[]{:S(2)}, u32[]{:S(2)}) %collective-permute-start.21) | collective-permute-done | bytes 589856 | tf_op jit(solution)/shard_map/ppermute | solution.py:145
  225.4 24.9 %collective-permute-done.22 = bf16[4,2,1,1,96,768]{5,4,0,3,2,1:T(8,128)(2,1)S(1)} collective-permute-done((bf16[4,2,1,1,96,768]{5,4,0,3,2,1:T(8,128)(2,1)S(1)}, bf16[4,2,1,1,96,768]{5,4,0,3,2,1:T(8,128)(2,1)S(1)}, u32[]{:S(2)}, u32[]{:S(2)}) %collective-permute-start.22) | collective-permute-done | bytes 1179680 | tf_op jit(solution)/shard_map/ppermute | solution.py:145
  253.1 1.8 copy.60
  254.9 1.8 copy.57
  257.1 2.0 broadcast_select_fusion.1
  259.9 2.2 slice-done.4
  264.0 6.7 %convert_reduce_fusion = (f32[4,768]{1,0:T(4,128)S(1)}, bf16[4,512,768]{2,1,0:T(8,128)(2,1)S(1)}) fusion(f32[4,768,512]{1,2,0:T(8,128)S(1)} %bitcast.314, f32[4,768]{1,0:T(4,128)S(1)} %copy-done.59, bf16[4,768,768]{2,1,0:T(8,128)(2,1)S(1)} %bitcast.270, bf16[512,768]{1,0:T(8,128)(2,1)S(1)} %copy-done.32), kind=kOutput, calls=%fused_computation.16 | convolution fusion | flops 2452091904 | bytes 14966784 | tf_op jit(solution)/shard_map/nd,jdf->jnf/dot_general | solution.py:299
  270.7 2.9 fusion.23
  276.1 2.1 fusion.26
  278.1 4.6 %convolution_convert_fusion.1 = bf16[4,768,768]{1,2,0:T(8,128)(2,1)} fusion(bf16[4,512,768]{2,1,0:T(8,128)(2,1)S(1)} %get-tuple-element.139, f32[512,768]{1,0:T(8,128)S(1)} %copy-done.5, f32[768]{0:T(1024)S(1)} %copy-done.68, f32[768]{0:T(1024)S(1)} %copy-done.58, f32[512]{0:T(512)S(1)} %fusion.49, f32[512]{0:T(512)S(1)} %broadcast_multiply_fusion), kind=kOutput, calls=%fused_computation.25 | convolution fusion | flops 2420244480 | bytes 9447424 | tf_op jit(solution)/shard_map/nd,jnf->jdf/dot_general | solution.py:304
  283.5 5.5 %reshape.220 = bf16[4,2,2,2,96,192]{4,3,2,1,5,0:T(2,128)(2,1)S(1)} reshape(bf16[4,768,192]{1,2,0:T(8,128)(2,1)} %fusion.26) | data formatting | bytes 2359296 | tf_op jit(solution)/shard_map/reshape | solution.py:168
  289.0 4.4 constant_dynamic-slice_fusion.9
  294.7 3.3 constant_dynamic-slice_fusion.5
  301.5 16.5 %shard_map.297 = bf16[2,3,3,64,1024]{4,3,2,1,0:T(8,128)(2,1)S(1)} custom-call(bf16[2,3,3,64,1024]{4,3,2,1,0:T(8,128)(2,1)S(1)} %bitcast.261, f32[2,3,1,1024]{3,2,1,0:T(1,128)S(1)} %get-tuple-element.20.lse_ref, bf16[2,3,64,1024]{3,2,1,0:T(8,128)(2,1)S(1)} %bitcast.258), custom_call_target="tpu_custom_call" | custom-call | flops 4026531840 | bytes 5505024 | tf_op jit(solution)/shard_map/pallas_call | solution.py:123
  317.9 2.4 bitcast_convert_fusion
  322.4 2.0 collective-permute-start.25
  324.4 3.2 convert_bitcast_fusion
  327.6 3.9 copy.58
  349.6 2.3 fusion.19
  352.0 3.4 convert_reduce_fusion.3
  355.5 1.8 collective-permute-start.49
  357.5 1.8 collective-permute-done.49
  359.2 1.8 collective-permute-start.50
  366.6 1.8 collective-permute-start.33
  368.5 9.1 %fusion.25 = bf16[512,768]{1,0:T(8,128)(2,1)} fusion(f32[512,768]{1,0:T(8,128)S(1)} %copy-done.6, bf16[4,768,768]{2,1,0:T(8,128)(2,1)} %bitcast.271, f32[768]{0:T(1024)S(1)} %copy-done.67, f32[4,768,512]{1,2,0:T(8,128)} %copy-done.70, f32[4,768]{1,0:T(4,128)S(1)} %copy-done.60), kind=kOutput, calls=%fused_computation.64 | convolution fusion | flops 2432827392 | bytes 13384704 | tf_op jit(solution)/shard_map/jnf,jdf->nd/dot_general | solution.py:296
  377.5 1.8 collective-permute-start.55
  380.2 3.7 collective-permute-done.52
  388.0 2.4 add_convert_fusion.1
  392.9 7.6 %collective-permute-done.27 = bf16[2,1,2,1,96,576]{5,4,3,2,1,0:T(8,128)(2,1)S(1)} collective-permute-done((bf16[2,1,2,1,96,576]{5,4,3,2,1,0:T(8,128)(2,1)S(1)}, bf16[2,1,2,1,96,576]{5,4,3,2,1,0:T(8,128)(2,1)S(1)}, u32[]{:S(2)}, u32[]{:S(2)}) %collective-permute-start.27) | collective-permute-done | bytes 442400 | tf_op jit(solution)/shard_map/ppermute | solution.py:145
  402.2 4.7 %collective-permute-done.28 = bf16[2,1,1,1,96,576]{5,4,3,2,1,0:T(8,128)(2,1)S(1)} collective-permute-done((bf16[2,1,1,1,96,576]{5,4,3,2,1,0:T(8,128)(2,1)S(1)}, bf16[2,1,1,1,96,576]{5,4,3,2,1,0:T(8,128)(2,1)S(1)}, u32[]{:S(2)}, u32[]{:S(2)}) %collective-permute-start.28) | collective-permute-done | bytes 221216 | tf_op jit(solution)/shard_map/ppermute | solution.py:145
  407.3 12.4 %collective-permute-done.37 = bf16[4,1,2,1,96,768]{5,4,3,2,1,0:T(8,128)(2,1)S(1)} collective-permute-done((bf16[4,1,2,1,96,768]{5,4,3,2,1,0:T(8,128)(2,1)S(1)}, bf16[4,1,2,1,96,768]{5,4,3,2,1,0:T(8,128)(2,1)S(1)}, u32[]{:S(2)}, u32[]{:S(2)}) %collective-permute-start.37) | collective-permute-done | bytes 1179680 | tf_op jit(solution)/shard_map/ppermute | solution.py:145
  422.5 7.6 %collective-permute-done.38 = bf16[4,1,1,1,96,768]{5,4,3,2,1,0:T(8,128)(2,1)} collective-permute-done((bf16[4,1,1,1,96,768]{5,4,3,2,1,0:T(8,128)(2,1)S(1)}, bf16[4,1,1,1,96,768]{5,4,3,2,1,0:T(8,128)(2,1)}, u32[]{:S(2)}, u32[]{:S(2)}) %collective-permute-start.38) | collective-permute-done | bytes 589856 | tf_op jit(solution)/shard_map/ppermute | solution.py:145
  439.4 4.1 collective-permute-done.40
  443.5 2.1 multiply_subtract_fusion.1
  (374 shorter events, 104.1 us)
Async XLA Ops:
  1.7 17.4 %collective-permute-start.8 = (bf16[96,192]{0,1:T(8,128)(2,1)S(1)}, bf16[96,192]{0,1:T(8,128)(2,1)S(1)}, u32[]{:S(2)}, u32[]{:S(2)}) collective-permute-start(bf16[96,192]{0,1:T(8,128)(2,1)S(1)} %get-tuple-element.112), channel_id=1, source_target_pairs={{0,3},{1,2},{2,1},{3,0},{4,7},{5,6},{6,5},{7,4},{8,11},{9,10},{10,... | collective-permute-start | bytes 110600 | tf_op jit(solution)/shard_map/ppermute | solution.py:145
  6.8 13.0 %collective-permute-start.7 = (bf16[96,192]{0,1:T(8,128)(2,1)S(1)}, bf16[96,192]{0,1:T(8,128)(2,1)S(1)}, u32[]{:S(2)}, u32[]{:S(2)}) collective-permute-start(bf16[96,192]{0,1:T(8,128)(2,1)S(1)} %get-tuple-element.112), channel_id=1, source_target_pairs={{0,2},{1,3},{2,0},{3,1},{4,6},{5,7},{6,4},{7,5},{8,10},{9,11},{10,... | collective-permute-start | bytes 110600 | tf_op jit(solution)/shard_map/ppermute | solution.py:145
  6.8 15.3 %collective-permute-start.6 = (bf16[96,192]{0,1:T(8,128)(2,1)S(1)}, bf16[96,192]{0,1:T(8,128)(2,1)S(1)}, u32[]{:S(2)}, u32[]{:S(2)}) collective-permute-start(bf16[96,192]{0,1:T(8,128)(2,1)S(1)} %get-tuple-element.112), channel_id=1, source_target_pairs={{0,1},{1,0},{2,3},{3,2},{4,5},{5,4},{6,7},{7,6},{8,9},{9,8},{10,11... | collective-permute-start | bytes 110600 | tf_op jit(solution)/shard_map/ppermute | solution.py:145
  9.1 23.1 %collective-permute-start.14 = (bf16[96,768]{1,0:T(8,128)(2,1)}, bf16[96,768]{1,0:T(8,128)(2,1)S(1)}, u32[]{:S(2)}, u32[]{:S(2)}) collective-permute-start(bf16[96,768]{1,0:T(8,128)(2,1)} %convert_element_type.249), channel_id=1, source_target_pairs={{0,3},{1,2},{2,1},{3,0},{4,7},{5,6},{6,5},{7,4},{8,11},{9,10},{10,... | collective-permute-start | bytes 442376 | tf_op jit(solution)/shard_map/ppermute | solution.py:145
  12.8 20.9 %collective-permute-start.13 = (bf16[96,768]{1,0:T(8,128)(2,1)}, bf16[96,768]{1,0:T(8,128)(2,1)S(1)}, u32[]{:S(2)}, u32[]{:S(2)}) collective-permute-start(bf16[96,768]{1,0:T(8,128)(2,1)} %convert_element_type.249), channel_id=1, source_target_pairs={{0,2},{1,3},{2,0},{3,1},{4,6},{5,7},{6,4},{7,5},{8,10},{9,11},{10,... | collective-permute-start | bytes 442376 | tf_op jit(solution)/shard_map/ppermute | solution.py:145
  19.1 14.6 %collective-permute-start.12 = (bf16[96,768]{1,0:T(8,128)(2,1)}, bf16[96,768]{1,0:T(8,128)(2,1)S(1)}, u32[]{:S(2)}, u32[]{:S(2)}) collective-permute-start(bf16[96,768]{1,0:T(8,128)(2,1)} %convert_element_type.249), channel_id=1, source_target_pairs={{0,1},{1,0},{2,3},{3,2},{4,5},{5,4},{6,7},{7,6},{8,9},{9,8},{10,11... | collective-permute-start | bytes 442376 | tf_op jit(solution)/shard_map/ppermute | solution.py:145
  19.7 10.6 %collective-permute-start = (bf16[96,576]{0,1:T(8,128)(2,1)S(1)}, bf16[96,576]{0,1:T(8,128)(2,1)S(1)}, u32[]{:S(2)}, u32[]{:S(2)}) collective-permute-start(bf16[96,576]{0,1:T(8,128)(2,1)S(1)} %bitcast.296), channel_id=1, source_target_pairs={{0,2},{1,3},{2,0},{3,1},{4,6},{5,7},{6,4},{7,5},{8,10},{9,11},{10,... | collective-permute-start | bytes 331784 | tf_op jit(solution)/shard_map/ppermute | solution.py:145
  22.1 36.9 %collective-permute-start.4 = (bf16[512,768]{1,0:T(8,128)(2,1)S(1)}, bf16[512,768]{1,0:T(8,128)(2,1)S(1)}, u32[]{:S(2)}, u32[]{:S(2)}) collective-permute-start(bf16[512,768]{1,0:T(8,128)(2,1)S(1)} %fusion.18), channel_id=1, source_target_pairs={{0,1},{1,0},{2,3},{3,2},{4,5},{5,4},{6,7},{7,6},{8,9},{9,8},{10,11... | collective-permute-start | bytes 2359304 | tf_op jit(solution)/shard_map/ppermute | solution.py:145
  30.3 6.0 %collective-permute-start.9 = (bf16[4,1,1,1,96,192]{4,5,0,3,2,1:T(8,128)(2,1)}, bf16[4,1,1,1,96,192]{4,5,0,3,2,1:T(8,128)(2,1)}, u32[]{:S(2)}, u32[]{:S(2)}) collective-permute-start(bf16[4,1,1,1,96,192]{4,5,0,3,2,1:T(8,128)(2,1)} %maximum_bitcast_fusion.5), channel_id=1, source_target_pairs={{0,16},{4,20},{8,24},{12,28},{16,0},{20,4},{24,8},{28,12},{1,17},{... | collective-permute-start | bytes 442376 | tf_op jit(solution)/shard_map/ppermute | solution.py:145
  32.1 9.0 %collective-permute-start.1 = (bf16[2,1,1,1,96,576]{5,4,0,3,2,1:T(8,128)(2,1)S(1)}, bf16[2,1,1,1,96,576]{5,4,0,3,2,1:T(8,128)(2,1)S(1)}, u32[]{:S(2)}, u32[]{:S(2)}) collective-permute-start(bf16[2,1,1,1,96,576]{5,4,0,3,2,1:T(8,128)(2,1)S(1)} %bitcast.279), channel_id=1, source_target_pairs={{0,8},{4,12},{8,0},{12,4},{16,24},{20,28},{24,16},{28,20},{1,9},{5... | collective-permute-start | bytes 663560 | tf_op jit(solution)/shard_map/ppermute | solution.py:145
  33.8 20.0 %collective-permute-start.15 = (bf16[4,1,1,1,96,768]{5,4,0,3,2,1:T(8,128)(2,1)S(1)}, bf16[4,1,1,1,96,768]{5,4,0,3,2,1:T(8,128)(2,1)S(1)}, u32[]{:S(2)}, u32[]{:S(2)}) collective-permute-start(bf16[4,1,1,1,96,768]{5,4,0,3,2,1:T(8,128)(2,1)S(1)} %maximum_bitcast_fusion.3), channel_id=1, source_target_pairs={{0,8},{4,12},{8,0},{12,4},{16,24},{20,28},{24,16},{28,20},{1,9},{5... | collective-permute-start | bytes 1769480 | tf_op jit(solution)/shard_map/ppermute | solution.py:145
  41.2 13.4 %collective-permute-start.2 = (bf16[2,1,2,1,96,576]{5,4,0,3,2,1:T(8,128)(2,1)S(1)}, bf16[2,1,2,1,96,576]{5,4,0,3,2,1:T(8,128)(2,1)S(1)}, u32[]{:S(2)}, u32[]{:S(2)}) collective-permute-start(bf16[2,1,2,1,96,576]{5,4,0,3,2,1:T(8,128)(2,1)S(1)} %pad_maximum_fusion.12), channel_id=1, source_target_pairs={{0,16},{4,20},{8,24},{12,28},{16,0},{20,4},{24,8},{28,12},{1,17},{... | collective-permute-start | bytes 1327112 | tf_op jit(solution)/shard_map/ppermute | solution.py:145
  41.9 16.7 %collective-permute-start.10 = (bf16[4,2,1,1,96,192]{4,5,0,3,2,1:T(8,128)(2,1)S(1)}, bf16[4,2,1,1,96,192]{4,5,0,3,2,1:T(8,128)(2,1)S(1)}, u32[]{:S(2)}, u32[]{:S(2)}) collective-permute-start(bf16[4,2,1,1,96,192]{4,5,0,3,2,1:T(8,128)(2,1)S(1)} %pad_maximum_fusion.13), channel_id=1, source_target_pairs={{0,8},{4,12},{8,0},{12,4},{16,24},{20,28},{24,16},{28,20},{1,9},{5... | collective-permute-start | bytes 884744 | tf_op jit(solution)/shard_map/ppermute | solution.py:145
  54.0 21.4 %collective-permute-start.16 = (bf16[4,1,2,1,96,768]{5,4,0,3,2,1:T(8,128)(2,1)S(1)}, bf16[4,1,2,1,96,768]{5,4,0,3,2,1:T(8,128)(2,1)S(1)}, u32[]{:S(2)}, u32[]{:S(2)}) collective-permute-start(bf16[4,1,2,1,96,768]{5,4,0,3,2,1:T(8,128)(2,1)S(1)} %pad_maximum_fusion.6), channel_id=1, source_target_pairs={{0,16},{4,20},{8,24},{12,28},{16,0},{20,4},{24,8},{28,12},{1,17},{... | collective-permute-start | bytes 3538952 | tf_op jit(solution)/shard_map/ppermute | solution.py:145
  54.9 4.7 %collective-permute-start.3 = (bf16[2,2,2,1,96,576]{5,4,0,3,2,1:T(8,128)(2,1)S(1)}, bf16[2,2,2,1,96,576]{5,4,0,3,2,1:T(8,128)(2,1)S(1)}, u32[]{:S(2)}, u32[]{:S(2)}) collective-permute-start(bf16[2,2,2,1,96,576]{5,4,0,3,2,1:T(8,128)(2,1)S(1)} %pad_maximum_fusion.8), channel_id=1, source_target_pairs={{0,4},{4,0},{8,12},{12,8},{16,20},{20,16},{24,28},{28,24},{1,5},{5... | collective-permute-start | bytes 2654216 | tf_op jit(solution)/shard_map/ppermute | solution.py:145
  58.9 38.3 %collective-permute-start.11 = (bf16[4,2,2,1,96,192]{4,5,0,3,2,1:T(8,128)(2,1)S(1)}, bf16[4,2,2,1,96,192]{4,5,0,3,2,1:T(8,128)(2,1)S(1)}, u32[]{:S(2)}, u32[]{:S(2)}) collective-permute-start(bf16[4,2,2,1,96,192]{4,5,0,3,2,1:T(8,128)(2,1)S(1)} %pad_maximum_fusion.10), channel_id=1, source_target_pairs={{0,4},{4,0},{8,12},{12,8},{16,20},{20,16},{24,28},{28,24},{1,5},{5... | collective-permute-start | bytes 1769480 | tf_op jit(solution)/shard_map/ppermute | solution.py:145
  59.6 18.2 %copy-start.27 = (bf16[512,768]{1,0:T(8,128)(2,1)}, bf16[512,768]{1,0:T(8,128)(2,1)S(1)}, u32[]{:S(2)}) copy-start(bf16[512,768]{1,0:T(8,128)(2,1)S(1)} %get-tuple-element.82) | copy-start | bytes 2359300
  77.2 32.9 %collective-permute-start.17 = (bf16[4,2,2,1,96,768]{5,4,0,3,2,1:T(8,128)(2,1)}, bf16[4,2,2,1,96,768]{5,4,0,3,2,1:T(8,128)(2,1)}, u32[]{:S(2)}, u32[]{:S(2)}) collective-permute-start(bf16[4,2,2,1,96,768]{5,4,0,3,2,1:T(8,128)(2,1)} %pad_maximum_fusion.2), channel_id=1, source_target_pairs={{0,4},{4,0},{8,12},{12,8},{16,20},{20,16},{24,28},{28,24},{1,5},{5... | collective-permute-start | bytes 7077896 | tf_op jit(solution)/shard_map/ppermute | solution.py:145
  95.3 12.0 %collective-permute-start.5 = (bf16[2,192,512]{2,1,0:T(8,128)(2,1)}, bf16[2,192,512]{2,1,0:T(8,128)(2,1)}, u32[]{:S(2)}, u32[]{:S(2)}) collective-permute-start(bf16[2,192,512]{2,1,0:T(8,128)(2,1)} %get-tuple-element.95), channel_id=1, source_target_pairs={{0,1},{1,0},{2,3},{3,2},{4,5},{5,4},{6,7},{7,6},{8,9},{9,8},{10,11... | collective-permute-start | bytes 1179656 | tf_op jit(solution)/shard_map/ppermute | solution.py:145
  124.1 4.7 %collective-permute-start.42 = (bf16[4,2,2,1,96,768]{5,4,3,2,1,0:T(8,128)(2,1)S(1)}, bf16[4,2,2,1,96,768]{5,4,3,2,1,0:T(8,128)(2,1)}, u32[]{:S(2)}, u32[]{:S(2)}) collective-permute-start(bf16[4,2,2,1,96,768]{5,4,3,2,1,0:T(8,128)(2,1)S(1)} %constant_dynamic-slice_fusion.2), channel_id=1, source_target_pairs={{0,4},{4,0},{8,12},{12,8},{16,20},{20,16},{24,28},{28,24},{1,5},{5... | collective-permute-start | bytes 7077896 | tf_op jit(solution)/shard_map/ppermute | solution.py:145
  133.0 28.3 %collective-permute-start.43 = (bf16[4,2,1,1,96,768]{5,4,3,2,1,0:T(8,128)(2,1)}, bf16[4,2,1,1,96,768]{5,4,3,2,1,0:T(8,128)(2,1)}, u32[]{:S(2)}, u32[]{:S(2)}) collective-permute-start(bf16[4,2,1,1,96,768]{5,4,3,2,1,0:T(8,128)(2,1)} %constant_dynamic-slice_fusion.1), channel_id=1, source_target_pairs={{0,8},{4,12},{8,0},{12,4},{16,24},{20,28},{24,16},{28,20},{1,9},{5... | collective-permute-start | bytes 3538952 | tf_op jit(solution)/shard_map/ppermute | solution.py:145
  163.9 30.8 %copy-start.37 = (f32[768,96]{0,1:T(8,128)S(1)}, f32[768,96]{0,1:T(8,128)}, u32[]{:S(2)}) copy-start(f32[768,96]{0,1:T(8,128)} %param.22) | copy-start | bytes 884740
  163.9 30.8 %copy-start.38 = (f32[768,96]{0,1:T(8,128)S(1)}, f32[768,96]{0,1:T(8,128)}, u32[]{:S(2)}) copy-start(f32[768,96]{0,1:T(8,128)} %param.31) | copy-start | bytes 884740
  164.0 30.8 %copy-start.39 = (f32[768,96]{0,1:T(8,128)S(1)}, f32[768,96]{0,1:T(8,128)}, u32[]{:S(2)}) copy-start(f32[768,96]{0,1:T(8,128)} %param.30) | copy-start | bytes 884740
  164.0 14.6 %collective-permute-start.44 = (bf16[4,1,1,1,96,768]{5,4,3,2,1,0:T(8,128)(2,1)S(1)}, bf16[4,1,1,1,96,768]{5,4,3,2,1,0:T(8,128)(2,1)S(1)}, u32[]{:S(2)}, u32[]{:S(2)}) collective-permute-start(bf16[4,1,1,1,96,768]{5,4,3,2,1,0:T(8,128)(2,1)S(1)} %constant_dynamic-slice_fusion), channel_id=1, source_target_pairs={{0,16},{4,20},{8,24},{12,28},{16,0},{20,4},{24,8},{28,12},{1,17},{... | collective-permute-start | bytes 1769480 | tf_op jit(solution)/shard_map/ppermute | solution.py:145
  179.8 8.6 %collective-permute-start.47 = (bf16[96,768]{1,0:T(8,128)(2,1)S(1)}, bf16[96,768]{1,0:T(8,128)(2,1)S(1)}, u32[]{:S(2)}, u32[]{:S(2)}) collective-permute-start(bf16[96,768]{1,0:T(8,128)(2,1)S(1)} %get-tuple-element.97), channel_id=1, source_target_pairs={{0,3},{1,2},{2,1},{3,0},{4,7},{5,6},{6,5},{7,4},{8,11},{9,10},{10,... | collective-permute-start | bytes 442376 | tf_op jit(solution)/shard_map/ppermute | solution.py:145
  183.0 11.7 %collective-permute-start.46 = (bf16[96,768]{1,0:T(8,128)(2,1)S(1)}, bf16[96,768]{1,0:T(8,128)(2,1)S(1)}, u32[]{:S(2)}, u32[]{:S(2)}) collective-permute-start(bf16[96,768]{1,0:T(8,128)(2,1)S(1)} %get-tuple-element.98), channel_id=1, source_target_pairs={{0,2},{1,3},{2,0},{3,1},{4,6},{5,7},{6,4},{7,5},{8,10},{9,11},{10,... | collective-permute-start | bytes 442376 | tf_op jit(solution)/shard_map/ppermute | solution.py:145
  183.1 11.6 %collective-permute-start.45 = (bf16[96,768]{1,0:T(8,128)(2,1)S(1)}, bf16[96,768]{1,0:T(8,128)(2,1)S(1)}, u32[]{:S(2)}, u32[]{:S(2)}) collective-permute-start(bf16[96,768]{1,0:T(8,128)(2,1)S(1)} %get-tuple-element.96), channel_id=1, source_target_pairs={{0,1},{1,0},{2,3},{3,2},{4,5},{5,4},{6,7},{7,6},{8,9},{9,8},{10,11... | collective-permute-start | bytes 442376 | tf_op jit(solution)/shard_map/ppermute | solution.py:145
  195.8 8.6 %collective-permute-start.20 = (bf16[96,768]{1,0:T(8,128)(2,1)S(1)}, bf16[96,768]{1,0:T(8,128)(2,1)S(1)}, u32[]{:S(2)}, u32[]{:S(2)}) collective-permute-start(bf16[96,768]{1,0:T(8,128)(2,1)S(1)} %get-tuple-element.107), channel_id=1, source_target_pairs={{0,3},{1,2},{2,1},{3,0},{4,7},{5,6},{6,5},{7,4},{8,11},{9,10},{10,... | collective-permute-start | bytes 442376 | tf_op jit(solution)/shard_map/ppermute | solution.py:145
  197.5 11.2 %collective-permute-start.19 = (bf16[96,768]{1,0:T(8,128)(2,1)S(1)}, bf16[96,768]{1,0:T(8,128)(2,1)S(1)}, u32[]{:S(2)}, u32[]{:S(2)}) collective-permute-start(bf16[96,768]{1,0:T(8,128)(2,1)S(1)} %get-tuple-element.107), channel_id=1, source_target_pairs={{0,2},{1,3},{2,0},{3,1},{4,6},{5,7},{6,4},{7,5},{8,10},{9,11},{10,... | collective-permute-start | bytes 442376 | tf_op jit(solution)/shard_map/ppermute | solution.py:145
  197.5 11.2 %collective-permute-start.18 = (bf16[96,768]{1,0:T(8,128)(2,1)S(1)}, bf16[96,768]{1,0:T(8,128)(2,1)S(1)}, u32[]{:S(2)}, u32[]{:S(2)}) collective-permute-start(bf16[96,768]{1,0:T(8,128)(2,1)S(1)} %get-tuple-element.107), channel_id=1, source_target_pairs={{0,1},{1,0},{2,3},{3,2},{4,5},{5,4},{6,7},{7,6},{8,9},{9,8},{10,11... | collective-permute-start | bytes 442376 | tf_op jit(solution)/shard_map/ppermute | solution.py:145
  208.9 14.8 %collective-permute-start.21 = (bf16[4,1,1,1,96,768]{5,4,0,3,2,1:T(8,128)(2,1)S(1)}, bf16[4,1,1,1,96,768]{5,4,0,3,2,1:T(8,128)(2,1)S(1)}, u32[]{:S(2)}, u32[]{:S(2)}) collective-permute-start(bf16[4,1,1,1,96,768]{5,4,0,3,2,1:T(8,128)(2,1)S(1)} %maximum_bitcast_fusion.4), channel_id=1, source_target_pairs={{0,16},{4,20},{8,24},{12,28},{16,0},{20,4},{24,8},{28,12},{1,17},{... | collective-permute-start | bytes 1769480 | tf_op jit(solution)/shard_map/ppermute | solution.py:145
  223.9 26.5 %collective-permute-start.22 = (bf16[4,2,1,1,96,768]{5,4,0,3,2,1:T(8,128)(2,1)S(1)}, bf16[4,2,1,1,96,768]{5,4,0,3,2,1:T(8,128)(2,1)S(1)}, u32[]{:S(2)}, u32[]{:S(2)}) collective-permute-start(bf16[4,2,1,1,96,768]{5,4,0,3,2,1:T(8,128)(2,1)S(1)} %pad_maximum_fusion.7), channel_id=1, source_target_pairs={{0,8},{4,12},{8,0},{12,4},{16,24},{20,28},{24,16},{28,20},{1,9},{5... | collective-permute-start | bytes 3538952 | tf_op jit(solution)/shard_map/ppermute | solution.py:145
  252.2 4.9 %collective-permute-start.23 = (bf16[4,2,2,1,96,768]{5,4,0,3,2,1:T(8,128)(2,1)}, bf16[4,2,2,1,96,768]{5,4,0,3,2,1:T(8,128)(2,1)}, u32[]{:S(2)}, u32[]{:S(2)}) collective-permute-start(bf16[4,2,2,1,96,768]{5,4,0,3,2,1:T(8,128)(2,1)} %pad_maximum_fusion.3), channel_id=1, source_target_pairs={{0,4},{4,0},{8,12},{12,8},{16,20},{20,16},{24,28},{28,24},{1,5},{5... | collective-permute-start | bytes 7077896 | tf_op jit(solution)/shard_map/ppermute | solution.py:145
  283.5 16.2 %collective-permute-start.24 = (bf16[2,192,512]{2,1,0:T(8,128)(2,1)}, bf16[2,192,512]{2,1,0:T(8,128)(2,1)}, u32[]{:S(2)}, u32[]{:S(2)}) collective-permute-start(bf16[2,192,512]{2,1,0:T(8,128)(2,1)} %slice_bitcast_fusion), channel_id=1, source_target_pairs={{0,1},{1,0},{2,3},{3,2},{4,5},{5,4},{6,7},{7,6},{8,9},{9,8},{10,11... | collective-permute-start | bytes 1179656 | tf_op jit(solution)/shard_map/ppermute | solution.py:145
  294.5 38.0 %collective-permute-start.30 = (bf16[4,2,2,1,96,192]{4,5,3,2,1,0:T(8,128)(2,1)}, bf16[4,2,2,1,96,192]{4,5,3,2,1,0:T(8,128)(2,1)}, u32[]{:S(2)}, u32[]{:S(2)}) collective-permute-start(bf16[4,2,2,1,96,192]{4,5,3,2,1,0:T(8,128)(2,1)} %copy.79), channel_id=1, source_target_pairs={{0,4},{4,0},{8,12},{12,8},{16,20},{20,16},{24,28},{28,24},{1,5},{5... | collective-permute-start | bytes 1769480 | tf_op jit(solution)/shard_map/ppermute | solution.py:145
  297.9 90.0 %collective-permute-start.36 = (bf16[4,2,2,1,96,768]{5,4,3,2,1,0:T(8,128)(2,1)}, bf16[4,2,2,1,96,768]{5,4,3,2,1,0:T(8,128)(2,1)}, u32[]{:S(2)}, u32[]{:S(2)}) collective-permute-start(bf16[4,2,2,1,96,768]{5,4,3,2,1,0:T(8,128)(2,1)} %constant_dynamic-slice_fusion.5), channel_id=1, source_target_pairs={{0,4},{4,0},{8,12},{12,8},{16,20},{20,16},{24,28},{28,24},{1,5},{5... | collective-permute-start | bytes 7077896 | tf_op jit(solution)/shard_map/ppermute | solution.py:145
  322.4 25.4 %collective-permute-start.25 = (bf16[512,768]{1,0:T(8,128)(2,1)}, bf16[512,768]{1,0:T(8,128)(2,1)}, u32[]{:S(2)}, u32[]{:S(2)}) collective-permute-start(bf16[512,768]{1,0:T(8,128)(2,1)} %constant_dynamic-slice_fusion.13), channel_id=1, source_target_pairs={{0,1},{1,0},{2,3},{3,2},{4,5},{5,4},{6,7},{7,6},{8,9},{9,8},{10,11... | collective-permute-start | bytes 2359304 | tf_op jit(solution)/shard_map/ppermute | solution.py:145
  335.2 11.1 %collective-permute-start.31 = (bf16[4,2,1,1,96,192]{4,5,3,2,1,0:T(8,128)(2,1)}, bf16[4,2,1,1,96,192]{4,5,3,2,1,0:T(8,128)(2,1)}, u32[]{:S(2)}, u32[]{:S(2)}) collective-permute-start(bf16[4,2,1,1,96,192]{4,5,3,2,1,0:T(8,128)(2,1)} %constant_dynamic-slice_fusion.7), channel_id=1, source_target_pairs={{0,8},{4,12},{8,0},{12,4},{16,24},{20,28},{24,16},{28,20},{1,9},{5... | collective-permute-start | bytes 884744 | tf_op jit(solution)/shard_map/ppermute | solution.py:145
  337.8 46.9 %collective-permute-start.26 = (bf16[2,2,2,1,96,576]{5,4,3,2,1,0:T(8,128)(2,1)}, bf16[2,2,2,1,96,576]{5,4,3,2,1,0:T(8,128)(2,1)}, u32[]{:S(2)}, u32[]{:S(2)}) collective-permute-start(bf16[2,2,2,1,96,576]{5,4,3,2,1,0:T(8,128)(2,1)} %constant_dynamic-slice_fusion.12), channel_id=1, source_target_pairs={{0,4},{4,0},{8,12},{12,8},{16,20},{20,16},{24,28},{28,24},{1,5},{5... | collective-permute-start | bytes 2654216 | tf_op jit(solution)/shard_map/ppermute | solution.py:145
  347.5 13.5 %collective-permute-start.32 = (bf16[4,1,1,1,96,192]{4,5,3,2,1,0:T(8,128)(2,1)S(1)}, bf16[4,1,1,1,96,192]{4,5,3,2,1,0:T(8,128)(2,1)S(1)}, u32[]{:S(2)}, u32[]{:S(2)}) collective-permute-start(bf16[4,1,1,1,96,192]{4,5,3,2,1,0:T(8,128)(2,1)S(1)} %constant_dynamic-slice_fusion.6), channel_id=1, source_target_pairs={{0,16},{4,20},{8,24},{12,28},{16,0},{20,4},{24,8},{28,12},{1,17},{... | collective-permute-start | bytes 442376 | tf_op jit(solution)/shard_map/ppermute | solution.py:145
  351.9 3.5 collective-permute-start.48
  352.0 35.9 %slice-start = ((s8[4718592]{0:T(1024)(128)(4,1)}), s8[4194304]{0:T(1024)(128)(4,1)S(1)}, s32[]{:S(2)}) async-start(s8[4718592]{0:T(1024)(128)(4,1)} %bitcast.265), calls=%async_computation | async-start | bytes 8388608
  355.5 3.8 collective-permute-start.49
  357.3 3.8 collective-permute-start.53
  359.2 3.7 collective-permute-start.50
  361.1 3.9 collective-permute-start.54
  362.9 3.7 collective-permute-start.51
  363.9 13.6 %collective-permute-start.35 = (bf16[96,192]{0,1:T(8,128)(2,1)S(1)}, bf16[96,192]{0,1:T(8,128)(2,1)S(1)}, u32[]{:S(2)}, u32[]{:S(2)}) collective-permute-start(bf16[96,192]{0,1:T(8,128)(2,1)S(1)} %get-tuple-element.109), channel_id=1, source_target_pairs={{0,3},{1,2},{2,1},{3,0},{4,7},{5,6},{6,5},{7,4},{8,11},{9,10},{10,... | collective-permute-start | bytes 110600 | tf_op jit(solution)/shard_map/ppermute | solution.py:145
  365.0 14.4 %collective-permute-start.34 = (bf16[96,192]{0,1:T(8,128)(2,1)S(1)}, bf16[96,192]{0,1:T(8,128)(2,1)S(1)}, u32[]{:S(2)}, u32[]{:S(2)}) collective-permute-start(bf16[96,192]{0,1:T(8,128)(2,1)S(1)} %get-tuple-element.110), channel_id=1, source_target_pairs={{0,2},{1,3},{2,0},{3,1},{4,6},{5,7},{6,4},{7,5},{8,10},{9,11},{10,... | collective-permute-start | bytes 110600 | tf_op jit(solution)/shard_map/ppermute | solution.py:145
  366.6 12.8 %collective-permute-start.33 = (bf16[96,192]{0,1:T(8,128)(2,1)S(1)}, bf16[96,192]{0,1:T(8,128)(2,1)S(1)}, u32[]{:S(2)}, u32[]{:S(2)}) collective-permute-start(bf16[96,192]{0,1:T(8,128)(2,1)S(1)} %get-tuple-element.108), channel_id=1, source_target_pairs={{0,1},{1,0},{2,3},{3,2},{4,5},{5,4},{6,7},{7,6},{8,9},{9,8},{10,11... | collective-permute-start | bytes 110600 | tf_op jit(solution)/shard_map/ppermute | solution.py:145
  368.4 19.5 %slice-start.1 = ((s8[4718592]{0:T(1024)(128)(4,1)}), s8[524288]{0:T(1024)(128)(4,1)S(1)}, s32[]{:S(2)}) async-start(s8[4718592]{0:T(1024)(128)(4,1)} %bitcast.265), calls=%async_computation.1 | async-start | bytes 1048576
  377.5 6.4 %collective-permute-start.55 = (f32[6144]{0:T(1024)S(1)}, f32[6144]{0:T(1024)S(1)}, u32[]{:S(2)}, u32[]{:S(2)}) collective-permute-start(f32[6144]{0:T(1024)S(1)} %add.509), channel_id=1, source_target_pairs={{0,16},{4,20},{8,24},{12,28},{16,0},{20,4},{24,8},{28,12},{1,17},{... | collective-permute-start | bytes 73736 | tf_op jit(solution)/shard_map/ppermute | solution.py:145
  379.4 4.6 %collective-permute-start.52 = (f32[3072]{0:T(1024)S(1)}, f32[3072]{0:T(1024)S(1)}, u32[]{:S(2)}, u32[]{:S(2)}) collective-permute-start(f32[3072]{0:T(1024)S(1)} %add.502), channel_id=1, source_target_pairs={{0,2},{1,3},{2,0},{3,1},{4,6},{5,7},{6,4},{7,5},{8,10},{9,11},{10,... | collective-permute-start | bytes 36872 | tf_op jit(solution)/shard_map/ppermute | solution.py:145
  384.0 3.9 collective-permute-start.56
  386.3 14.2 %collective-permute-start.27 = (bf16[2,1,2,1,96,576]{5,4,3,2,1,0:T(8,128)(2,1)S(1)}, bf16[2,1,2,1,96,576]{5,4,3,2,1,0:T(8,128)(2,1)S(1)}, u32[]{:S(2)}, u32[]{:S(2)}) collective-permute-start(bf16[2,1,2,1,96,576]{5,4,3,2,1,0:T(8,128)(2,1)S(1)} %constant_dynamic-slice_fusion.11), channel_id=1, source_target_pairs={{0,16},{4,20},{8,24},{12,28},{16,0},{20,4},{24,8},{28,12},{1,17},{... | collective-permute-start | bytes 1327112 | tf_op jit(solution)/shard_map/ppermute | solution.py:145
  387.9 5.0 %collective-permute-start.57 = (f32[6144]{0:T(1024)S(1)}, f32[6144]{0:T(1024)S(1)}, u32[]{:S(2)}, u32[]{:S(2)}) collective-permute-start(f32[6144]{0:T(1024)S(1)} %add.511), channel_id=1, source_target_pairs={{0,2},{1,3},{2,0},{3,1},{4,6},{5,7},{6,4},{7,5},{8,10},{9,11},{10,... | collective-permute-start | bytes 73736 | tf_op jit(solution)/shard_map/ppermute | solution.py:145
  390.5 29.2 %collective-permute-start.37 = (bf16[4,1,2,1,96,768]{5,4,3,2,1,0:T(8,128)(2,1)S(1)}, bf16[4,1,2,1,96,768]{5,4,3,2,1,0:T(8,128)(2,1)S(1)}, u32[]{:S(2)}, u32[]{:S(2)}) collective-permute-start(bf16[4,1,2,1,96,768]{5,4,3,2,1,0:T(8,128)(2,1)S(1)} %constant_dynamic-slice_fusion.4), channel_id=1, source_target_pairs={{0,16},{4,20},{8,24},{12,28},{16,0},{20,4},{24,8},{28,12},{1,17},{... | collective-permute-start | bytes 3538952 | tf_op jit(solution)/shard_map/ppermute | solution.py:145
  400.7 6.3 %collective-permute-start.28 = (bf16[2,1,1,1,96,576]{5,4,3,2,1,0:T(8,128)(2,1)S(1)}, bf16[2,1,1,1,96,576]{5,4,3,2,1,0:T(8,128)(2,1)S(1)}, u32[]{:S(2)}, u32[]{:S(2)}) collective-permute-start(bf16[2,1,1,1,96,576]{5,4,3,2,1,0:T(8,128)(2,1)S(1)} %constant_dynamic-slice_fusion.10), channel_id=1, source_target_pairs={{0,8},{4,12},{8,0},{12,4},{16,24},{20,28},{24,16},{28,20},{1,9},{5... | collective-permute-start | bytes 663560 | tf_op jit(solution)/shard_map/ppermute | solution.py:145
  407.1 15.3 %collective-permute-start.29 = (bf16[96,576]{1,0:T(8,128)(2,1)S(1)}, bf16[96,576]{1,0:T(8,128)(2,1)S(1)}, u32[]{:S(2)}, u32[]{:S(2)}) collective-permute-start(bf16[96,576]{1,0:T(8,128)(2,1)S(1)} %slice_bitcast_fusion.10), channel_id=1, source_target_pairs={{0,2},{1,3},{2,0},{3,1},{4,6},{5,7},{6,4},{7,5},{8,10},{9,11},{10,... | collective-permute-start | bytes 331784 | tf_op jit(solution)/shard_map/ppermute | solution.py:145
  420.1 10.1 %collective-permute-start.38 = (bf16[4,1,1,1,96,768]{5,4,3,2,1,0:T(8,128)(2,1)S(1)}, bf16[4,1,1,1,96,768]{5,4,3,2,1,0:T(8,128)(2,1)}, u32[]{:S(2)}, u32[]{:S(2)}) collective-permute-start(bf16[4,1,1,1,96,768]{5,4,3,2,1,0:T(8,128)(2,1)S(1)} %constant_dynamic-slice_fusion.3), channel_id=1, source_target_pairs={{0,8},{4,12},{8,0},{12,4},{16,24},{20,28},{24,16},{28,20},{1,9},{5... | collective-permute-start | bytes 1769480 | tf_op jit(solution)/shard_map/ppermute | solution.py:145
  432.1 7.3 %collective-permute-start.41 = (bf16[96,768]{1,0:T(8,128)(2,1)}, bf16[96,768]{1,0:T(8,128)(2,1)S(1)}, u32[]{:S(2)}, u32[]{:S(2)}) collective-permute-start(bf16[96,768]{1,0:T(8,128)(2,1)} %get-tuple-element.100), channel_id=1, source_target_pairs={{0,3},{1,2},{2,1},{3,0},{4,7},{5,6},{6,5},{7,4},{8,11},{9,10},{10,... | collective-permute-start | bytes 442376 | tf_op jit(solution)/shard_map/ppermute | solution.py:145
  433.7 9.8 %collective-permute-start.40 = (bf16[96,768]{1,0:T(8,128)(2,1)}, bf16[96,768]{1,0:T(8,128)(2,1)}, u32[]{:S(2)}, u32[]{:S(2)}) collective-permute-start(bf16[96,768]{1,0:T(8,128)(2,1)} %get-tuple-element.101), channel_id=1, source_target_pairs={{0,2},{1,3},{2,0},{3,1},{4,6},{5,7},{6,4},{7,5},{8,10},{9,11},{10,... | collective-permute-start | bytes 442376 | tf_op jit(solution)/shard_map/ppermute | solution.py:145
  435.3 8.2 %collective-permute-start.39 = (bf16[96,768]{1,0:T(8,128)(2,1)}, bf16[96,768]{1,0:T(8,128)(2,1)}, u32[]{:S(2)}, u32[]{:S(2)}) collective-permute-start(bf16[96,768]{1,0:T(8,128)(2,1)} %get-tuple-element.99), channel_id=1, source_target_pairs={{0,1},{1,0},{2,3},{3,2},{4,5},{5,4},{6,7},{7,6},{8,9},{9,8},{10,11... | collective-permute-start | bytes 442376 | tf_op jit(solution)/shard_map/ppermute | solution.py:145
  (71 other events, 432.3 us)

commit v2 on v1

--- a/solution.py
+++ b/solution.py
@@ -3,6 +3,7 @@
 from jax import lax
 from jax.experimental import pallas as pl
 from jax.experimental.pallas import tpu as pltpu
+from jax.experimental.layout import Layout, with_layout_constraint
 from jax.sharding import PartitionSpec as P
 
 D = 768
@@ -149,23 +150,35 @@
     return lax.rem(lax.axis_index(axis_name) // (1 << bit), 2)
 
 
-def gather_data(values, order):
-    bits = len(order)
+def row_major(values):
+    return with_layout_constraint(values, Layout(tuple(range(values.ndim))))
+
+
+def gather_open(values, bits):
     blocks, rows, columns = values.shape
-    values = values.reshape((blocks,) + (1,) * bits + (rows, columns))
+    return values.reshape((blocks,) + (1,) * bits + (rows, columns))
+
+
+def gather_steps(values, bits, order):
     for bit in order:
         other = swap(values, "dp", 1 << bit)
         low = bit_of("dp", bit) == 0
         values = jnp.concatenate(
             [jnp.where(low, values, other), jnp.where(low, other, values)], axis=bits - bit
         )
-    return values.reshape(blocks, rows << bits, columns)
-
-
-def scatter_data(values, order):
-    bits = len(order)
+    return values
+
+
+def gather_close(values):
+    return values.reshape(values.shape[0], -1, values.shape[-1])
+
+
+def scatter_open(values, bits):
     blocks, rows, columns = values.shape
-    values = values.reshape((blocks,) + (2,) * bits + (rows >> bits, columns))
+    return row_major(values).reshape((blocks,) + (2,) * bits + (rows >> bits, columns))
+
+
+def scatter_steps(values, bits, order):
     for bit in order:
         mine = bit_of("dp", bit)
         axis = bits - bit
@@ -174,7 +187,11 @@
         )
         kept = lax.dynamic_index_in_dim(values, mine, axis, keepdims=True)
         values = (kept.astype(F32) + other.astype(F32)).astype(BF16)
-    return values.reshape(blocks, rows >> bits, columns)
+    return values
+
+
+def tie(*values):
+    return lax.optimization_barrier(values)
 
 
 def gather_blocks(shard, distances):
@@ -225,8 +242,7 @@
     n_tensor = lax.axis_size("tensor")
     bits = lax.axis_size("dp").bit_length() - 1
     outer = list(range(1, bits))
-    gather_one, gather_two = outer + [0], outer[::-1] + [0]
-    scatter_one, scatter_two = [0] + outer, [0] + outer[::-1]
+    near, far = outer, outer[::-1]
     rank = lax.axis_index("tensor")
     every = list(range(n_tensor))
     owned = every[::2]
@@ -261,21 +277,40 @@
         given = lax.dynamic_slice_in_dim(values, (1 - half) * rows, rows, axis)
         return kept, swap(given, "tensor", 1)
 
-    qkv_shard = w_qkv.astype(BF16).transpose(1, 0, 2).reshape(own_rows, 3 * head_cols)
-    qkv_full = gather_data(gather_blocks(qkv_shard, owned), gather_one)
-    out_full = gather_data(gather_blocks(w_out.astype(BF16).T, every), gather_two)
-    up_full = gather_data(gather_blocks(w_up.astype(BF16), every), gather_one)
-    down_full = gather_data(gather_blocks(w_down.astype(BF16).T, every), gather_two)
+    qkv_shard = row_major(w_qkv.astype(BF16).transpose(1, 0, 2).reshape(own_rows, 3 * head_cols))
+    up_out_shard = row_major(jnp.concatenate([w_up.astype(BF16), w_out.astype(BF16).T], axis=1))
+    down_shard = row_major(w_down.astype(BF16).T)
+    qkv_parts = gather_blocks(qkv_shard, owned)
+    qkv_full = gather_close(
+        jnp.concatenate(
+            [
+                gather_steps(gather_open(qkv_parts[:1], bits), bits, near + [0]),
+                gather_steps(gather_open(qkv_parts[1:], bits), bits, far + [0]),
+            ]
+        )
+    )
+    up_out = gather_open(gather_blocks(up_out_shard, every), bits)
+    down_full = gather_open(gather_blocks(down_shard, every), bits)
+    qkv_full, up_out, down_full = tie(qkv_full, up_out, down_full)
+    up_out = gather_steps(up_out, bits, near[:1])
+    down_full = gather_steps(down_full, bits, far[:1])
 
     query_bias = ranked(6 * width, head_cols, owned)
     value_bias = ranked(7 * width, head_cols, owned)
     biases = jnp.concatenate([query_bias, jnp.zeros_like(query_bias), value_bias], axis=1)
     projected = jnp.einsum("jde,nd->jen", qkv_full, normed_pair, preferred_element_type=F32)
     projected = (projected + biases[:, :, None]).astype(BF16)
+    projected, up_out, down_full = tie(projected, up_out, down_full)
+    up_out = gather_steps(up_out, bits, near[1:])
+    down_full = gather_steps(down_full, bits, far[1:])
     heads = head_cols // HEAD
     split = projected.reshape(len(owned), 3, heads, HEAD, 2 * rows)
     attended, log_sums = attend_forward(split)
     attended = attended.reshape(len(owned), head_cols, 2 * rows)
+    attended, up_out, down_full = tie(attended, up_out, down_full)
+    up_out = gather_close(gather_steps(up_out, bits, [0]))
+    down_full = gather_close(gather_steps(down_full, bits, [0]))
+    up_full, out_full = up_out[:, :, :unit_cols], up_out[:, :, unit_cols:]
     attended_own, attended_got = exchange(attended, 2)
     attended_all = jnp.stack([attended_own, attended_got], axis=1).reshape(
         n_tensor, head_cols, rows
@@ -283,7 +318,7 @@
     branch = jnp.einsum("jen,jde->nd", attended_all, out_full, preferred_element_type=F32)
     hidden = token_rows + branch + vector(4)
     normed_two, norm_two_pull = jax.vjp(layer_norm, hidden, vector(2), vector(3))
-    normed_two = normed_two.astype(BF16)
+    normed_two, down_full = tie(normed_two.astype(BF16), down_full)
     up_bias = ranked(8 * width, unit_cols, every)
     pre_act = (
         jnp.einsum("nd,jdf->jnf", normed_two, up_full, preferred_element_type=F32)
@@ -305,6 +340,11 @@
         BF16
     )
     grad_normed_two = jnp.einsum("jnf,jdf->nd", grad_pre, up_full, preferred_element_type=F32)
+    down_sum = scatter_steps(scatter_open(grad_down, bits), bits, [0])
+    up_sum = scatter_steps(scatter_open(grad_up, bits), bits, [0])
+    grad_normed_two, down_sum, up_sum = tie(grad_normed_two, down_sum, up_sum)
+    down_sum = scatter_steps(down_sum, bits, near[:1])
+    up_sum = scatter_steps(up_sum, bits, far[:1])
     up_sums = jnp.sum(grad_pre.astype(F32), axis=1)
     grad_from_norm, grad_gain_two, grad_shift_two = norm_two_pull(grad_normed_two)
     grad_hidden = cot_rows + grad_from_norm
@@ -325,13 +365,22 @@
     grad_out_w = jnp.einsum(
         "nd,jen->jde", grad_low, attended_all, preferred_element_type=F32
     ).astype(BF16)
-    grad_down_own = scatter_blocks(scatter_data(grad_down, scatter_one), every)
-    grad_up_own = scatter_blocks(scatter_data(grad_up, scatter_two), every)
-    grad_out_own = scatter_blocks(scatter_data(grad_out_w, scatter_one), every)
+    grad_heads, down_sum, up_sum = tie(grad_heads, down_sum, up_sum)
+    down_sum = scatter_steps(down_sum, bits, near[1:])
+    up_sum = scatter_steps(up_sum, bits, far[1:])
     grad_split = attend_backward(
         split, log_sums, grad_heads.reshape(len(owned), heads, HEAD, 2 * rows)
     )
     grad_proj = grad_split.reshape(len(owned), 3 * head_cols, 2 * rows)
+    grad_proj, down_sum, up_sum = tie(grad_proj, down_sum, up_sum)
+    out_sum = scatter_steps(scatter_open(grad_out_w, bits), bits, [0] + near)
+
+    def own_sum(values, distances):
+        return scatter_blocks(values.reshape(values.shape[0], own_rows, -1), distances)
+
+    grad_down_own = own_sum(down_sum, every)
+    grad_up_own = own_sum(up_sum, every)
+    grad_out_own = own_sum(out_sum, every)
     grad_normed_pair = jnp.einsum(
         "jen,jde->nd", grad_proj, qkv_full, preferred_element_type=F32
     ).astype(BF16)
@@ -340,7 +389,13 @@
     grad_qkv_w = jnp.einsum(
         "nd,jen->jde", normed_pair, grad_proj, preferred_element_type=F32
     ).astype(BF16)
-    grad_qkv_own = scatter_blocks(scatter_data(grad_qkv_w, scatter_two), owned)
+    qkv_sums = jnp.concatenate(
+        [
+            scatter_steps(scatter_open(grad_qkv_w[:1], bits), bits, [0] + near),
+            scatter_steps(scatter_open(grad_qkv_w[1:], bits), bits, [0] + far),
+        ]
+    )
+    grad_qkv_own = own_sum(qkv_sums, owned)
     grad_from_first, grad_gain_one, grad_shift_one = norm_one_pull(grad_normed_one)
     grad_tokens = grad_hidden + grad_from_first
 

time: 453 us -> 411 us (0.907)
  waiting for transfers between devices: 192 us -> 157 us
  local copies, waits for them, and re-layouts: 65.9 us -> 48.7 us
  matrix products: 41.8 us -> 56.6 us
    ppermute x58, waiting for transfers between devices: 192 us -> 157 us  [swap(): lax.ppermute(values, axis_name, [(i, i ^ distance) for i in range(size)])]
    dot_general x1, matrix products: 6.68 us -> 18.5 us  [on_device(): jnp.einsum('nd,jdf->jnf', cotangent, down_full, preferred_element_type=F32)]
    reshape x2 -> x1, local copies, waits for them, and re-layouts: 11.1 us -> 0.16 us  [on_device(): w_qkv.astype(BF16).transpose(1, 0, 2).reshape(own_rows, 3 * head_cols)]
    dynamic_slice x12 -> x15, local copies, waits for them, and re-layouts: 11.1 us -> 8.99 us  [the longest x12 5.51 us: scatter_steps(): lax.dynamic_index_in_dim(values, 1 - mine, axis, keepdims=True)]
    unnamed x165 -> x145, local copies, waits for them, and re-layouts: 21.9 us -> 20.1 us
    convert_element_type x13 -> x15, other arithmetic: 15.7 us -> 16.4 us  [the longest x13 16.1 us: scatter_steps(): values = (kept.astype(F32) + other.astype(F32)).astype(BF16)]
  transfers between devices with their start and end apart: 58 -> 58, of which waited for: 30 -> 25; matrix products, arithmetic and copies ran while one was open for 22% -> 23% of each run, Pallas kernels for 7% -> 8%
where the time goes in v2:
time: 411 us; the launch traced here: 405 us
  waiting for transfers between devices  157 us (38%)
  starting transfers between devices  61 us (15%)
  matrix products  56.6 us (14%)
  local copies, waits for them, and re-layouts  48.7 us (12%)
  other arithmetic  47.7 us (12%)
  Pallas kernels  30.6 us (7%)
    ppermute x58, waiting for transfers between devices, swap(): lax.ppermute(values, axis_name, [(i, i ^ distance) for i in range(size)])  157 us
    ppermute x58, starting transfers between devices, swap(): lax.ppermute(values, axis_name, [(i, i ^ distance) for i in range(size)])  61 us
    unnamed x145, local copies, waits for them, and re-layouts  20.1 us
    dot_general x1, matrix products, on_device(): jnp.einsum('nd,jdf->jnf', cotangent, down_full, preferred_element_type=F32)  18.5 us
    pallas_call x1, Pallas kernels, attend_backward(): pl.pallas_call(backward_kernel, grid=(groups, heads), in_specs=[pl.BlockS...  16.5 us
    convert_element_type x13, other arithmetic, scatter_steps(): values = (kept.astype(F32) + other.astype(F32)).astype(BF16)  16.1 us
    pallas_call x1, Pallas kernels, attend_forward(): pl.pallas_call(forward_kernel, grid=(groups, heads), in_specs=[pl.BlockSp...  14.2 us
    dot_general x1, matrix products, on_device(): jnp.einsum('jnf,jdf->nd', active, down_full, preferred_element_type=F32)  9.09 us
  transfers between devices with their start and end apart: 58, of which 25 were waited for; matrix products, arithmetic and copies ran while one was open for 23% of the time, Pallas kernels for 8%

profile of v2, /device:TPU:0, one launch (start us, length us, event | category | flops | bytes accessed | tf_op | source)
XLA Modules:
  0.0 404.6 jit_solution(4074449877644881993)
XLA Ops:
  1.8 5.1 %collective-permute-start.12 = (bf16[96,768]{1,0:T(8,128)(2,1)S(1)}, bf16[96,768]{1,0:T(8,128)(2,1)S(1)}, u32[]{:S(2)}, u32[]{:S(2)}) collective-permute-start(bf16[96,768]{1,0:T(8,128)(2,1)S(1)} %get-tuple-element.183), channel_id=1, source_target_pairs={{0,3},{1,2},{2,1},{3,0},{4,7},{5,6},{6,5},{7,4},{8,11},{9,10},{10,... | collective-permute-start | bytes 442376 | tf_op jit(solution)/shard_map/ppermute | solution.py:146
  8.8 2.4 collective-permute-start.3
  14.1 10.5 %collective-permute-done.3 = bf16[96,576]{1,0:T(8,128)(2,1)S(1)} collective-permute-done((bf16[96,576]{1,0:T(8,128)(2,1)S(1)}, bf16[96,576]{1,0:T(8,128)(2,1)S(1)}, u32[]{:S(2)}, u32[]{:S(2)}) %collective-permute-start.3) | collective-permute-done | bytes 110624 | tf_op jit(solution)/shard_map/ppermute | solution.py:146
  24.6 2.8 collective-permute-start.9
  29.0 3.4 collective-permute-done.4
  34.0 4.6 %collective-permute-done.1 = bf16[1,1,2,1,96,576]{5,4,3,2,1,0:T(8,128)(2,1)S(1)} collective-permute-done((bf16[1,1,2,1,96,576]{5,4,3,2,1,0:T(8,128)(2,1)S(1)}, bf16[1,1,2,1,96,576]{5,4,3,2,1,0:T(8,128)(2,1)S(1)}, u32[]{:S(2)}, u32[]{:S(2)}) %collective-permute-start.1) | collective-permute-done | bytes 221216 | tf_op jit(solution)/shard_map/ppermute | solution.py:146
  40.3 4.6 %collective-permute-done.5 = bf16[1,2,1,1,96,576]{5,4,3,2,1,0:T(8,128)(2,1)S(1)} collective-permute-done((bf16[1,2,1,1,96,576]{5,4,3,2,1,0:T(8,128)(2,1)S(1)}, bf16[1,2,1,1,96,576]{5,4,3,2,1,0:T(8,128)(2,1)S(1)}, u32[]{:S(2)}, u32[]{:S(2)}) %collective-permute-start.5) | collective-permute-done | bytes 221216 | tf_op jit(solution)/shard_map/ppermute | solution.py:146
  47.6 8.2 %collective-permute-done.8 = bf16[96,960]{1,0:T(8,128)(2,1)S(1)} collective-permute-done((bf16[96,960]{1,0:T(8,128)(2,1)S(1)}, bf16[96,960]{1,0:T(8,128)(2,1)S(1)}, u32[]{:S(2)}, u32[]{:S(2)}) %collective-permute-start.8) | collective-permute-done | bytes 184352 | tf_op jit(solution)/shard_map/ppermute | solution.py:146
  57.8 1.6 collective-permute-start.15
  59.3 14.1 %collective-permute-done.13 = bf16[512,768]{1,0:T(8,128)(2,1)S(1)} collective-permute-done((bf16[512,768]{1,0:T(8,128)(2,1)S(1)}, bf16[512,768]{1,0:T(8,128)(2,1)S(1)}, u32[]{:S(2)}, u32[]{:S(2)}) %collective-permute-start.13) | collective-permute-done | bytes 786464 | tf_op jit(solution)/shard_map/ppermute | solution.py:146
  75.6 2.4 add_convert_fusion.2
  78.3 15.0 %collective-permute-done.14 = bf16[4,1,1,1,96,960]{5,4,0,3,2,1:T(8,128)(2,1)S(1)} collective-permute-done((bf16[4,1,1,1,96,960]{5,4,0,3,2,1:T(8,128)(2,1)S(1)}, bf16[4,1,1,1,96,960]{5,4,0,3,2,1:T(8,128)(2,1)S(1)}, u32[]{:S(2)}, u32[]{:S(2)}) %collective-permute-start.14) | collective-permute-done | bytes 737312 | tf_op jit(solution)/shard_map/ppermute | solution.py:146
  96.6 14.2 %shard_map.296 = (bf16[2,3,64,1024]{3,2,1,0:T(8,128)(2,1)S(1)}, f32[2,3,1,1024]{3,2,1,0:T(1,128)S(1)}) custom-call(bf16[2,3,3,64,1024]{4,3,2,1,0:T(8,128)(2,1)S(1)} %bitcast.225), custom_call_target="tpu_custom_call" | custom-call | flops 1610612736 | bytes 3145728 | tf_op jit(solution)/shard_map/pallas_call | solution.py:101
  110.8 9.5 %collective-permute-done.17 = bf16[4,2,1,1,96,768]{5,4,0,3,2,1:T(8,128)(2,1)S(1)} collective-permute-done((bf16[4,2,1,1,96,768]{5,4,0,3,2,1:T(8,128)(2,1)S(1)}, bf16[4,2,1,1,96,768]{5,4,0,3,2,1:T(8,128)(2,1)S(1)}, u32[]{:S(2)}, u32[]{:S(2)}) %collective-permute-start.17) | collective-permute-done | bytes 1179680 | tf_op jit(solution)/shard_map/ppermute | solution.py:146
  120.5 1.7 pad_maximum_fusion.3
  122.2 7.8 %collective-permute-done.16 = bf16[4,1,2,1,96,960]{5,4,0,3,2,1:T(8,128)(2,1)S(1)} collective-permute-done((bf16[4,1,2,1,96,960]{5,4,0,3,2,1:T(8,128)(2,1)S(1)}, bf16[4,1,2,1,96,960]{5,4,0,3,2,1:T(8,128)(2,1)S(1)}, u32[]{:S(2)}, u32[]{:S(2)}) %collective-permute-start.16) | collective-permute-done | bytes 1474592 | tf_op jit(solution)/shard_map/ppermute | solution.py:146
  130.1 2.0 pad_maximum_fusion.2
  134.3 10.5 %collective-permute-done.18 = bf16[2,192,512]{2,1,0:T(8,128)(2,1)S(1)} collective-permute-done((bf16[2,192,512]{2,1,0:T(8,128)(2,1)}, bf16[2,192,512]{2,1,0:T(8,128)(2,1)S(1)}, u32[]{:S(2)}, u32[]{:S(2)}) %collective-permute-start.18) | collective-permute-done | bytes 393248 | tf_op jit(solution)/shard_map/ppermute | solution.py:146
  145.9 3.0 broadcast_select_fusion.3
  149.4 2.5 copy.112
  151.9 3.3 broadcast_select_fusion.1
  159.9 2.6 fusion.13
  162.6 3.5 convolution_convert_fusion.1
  166.2 18.5 %convert_reduce_fusion = (f32[4,768]{1,0:T(4,128)S(1)}, bf16[4,512,768]{2,1,0:T(8,128)(2,1)S(1)}) fusion(f32[4,768,512]{1,2,0:T(8,128)S(1)} %fusion.13, f32[4,768]{1,0:T(4,128)S(1)} %pad_maximum_fusion.14, bf16[4,768,768]{2,1,0:T(8,128)(2,1)S(1)} %bitcast.243, bf16[512,768]{1,0:T(8,128)(2,1)S(1)} %copy-done.34), kind=kOutput, calls=%fused_computation.17 | convolution fusion | flops 2452091904 | bytes 14966784 | tf_op jit(solution)/shard_map/nd,jdf->jnf/dot_general | solution.py:334
  184.7 1.8 constant_dynamic-slice_fusion.18
  187.2 3.1 convolution_convert_fusion
  190.3 1.6 constant_dynamic-slice_fusion.17
  194.1 1.8 copy.124
  195.9 1.8 copy.118
  198.9 6.1 %fusion.29 = f32[512,768]{1,0:T(8,128)S(1)} fusion(bf16[4,512,768]{2,1,0:T(8,128)(2,1)} %copy-done.58, bf16[4,768,960]{2,1,0:T(8,128)(2,1)} %bitcast.230), kind=kOutput, calls=%fused_computation.74 | convolution fusion | flops 2415919104 | bytes 9437184 | tf_op jit(solution)/shard_map/jnf,jdf->nd/dot_general | solution.py:342
  205.0 9.1 %fusion.28 = bf16[512,768]{1,0:T(8,128)(2,1)} fusion(f32[512,768]{1,0:T(8,128)S(1)} %copy-done.3, bf16[4,768,768]{2,1,0:T(8,128)(2,1)} %bitcast.240, f32[768]{0:T(1024)S(1)} %get-tuple-element.202, f32[4,768,512]{1,2,0:T(8,128)} %copy-done.57, f32[4,768]{1,0:T(4,128)S(1)} %copy-done.54), kind=kOutput, calls=%fused_computation.64 | convolution fusion | flops 2432827392 | bytes 13384704 | tf_op jit(solution)/shard_map/jnf,jdf->nd/dot_general | solution.py:331
  214.1 3.9 add_convert_fusion.1
  218.1 3.8 add_convert_fusion
  226.4 2.3 copy.147
  229.2 3.4 convolution_convert_fusion.4
  235.8 2.4 copy.146
  238.1 1.7 add_convert_fusion.5
  243.2 28.3 %collective-permute-done.37 = bf16[4,2,1,1,96,192]{4,5,3,2,1,0:T(8,128)(2,1)S(1)} collective-permute-done((bf16[4,2,1,1,96,192]{4,5,3,2,1,0:T(8,128)(2,1)S(1)}, bf16[4,2,1,1,96,192]{4,5,3,2,1,0:T(8,128)(2,1)S(1)}, u32[]{:S(2)}, u32[]{:S(2)}) %collective-permute-start.37) | collective-permute-done | bytes 294944 | tf_op jit(solution)/shard_map/ppermute | solution.py:146
  274.4 2.9 collective-permute-done.38
  277.4 1.6 collective-permute-start.41
  281.9 1.8 add_convert_fusion.4
  287.1 16.5 %shard_map.297 = bf16[2,3,3,64,1024]{4,3,2,1,0:T(8,128)(2,1)S(1)} custom-call(bf16[2,3,3,64,1024]{4,3,2,1,0:T(8,128)(2,1)S(1)} %bitcast.226, f32[2,3,1,1024]{3,2,1,0:T(1,128)S(1)} %get-tuple-element.52.lse_ref, bf16[2,3,64,1024]{3,2,1,0:T(8,128)(2,1)S(1)} %bitcast.223), custom_call_target="tpu_custom_call" | custom-call | flops 4026531840 | bytes 5505024 | tf_op jit(solution)/shard_map/pallas_call | solution.py:124
  305.5 2.4 bitcast_convert_fusion
  307.9 3.2 convolution_convert_fusion.2
  313.5 2.7 copy.119
  322.4 1.8 slice_bitcast_fusion.7
  324.2 1.9 collective-permute-start.44
  330.9 2.2 collective-permute-done.44
  333.1 2.0 collective-permute-start.47
  335.1 9.7 %collective-permute-done.43 = bf16[96,768]{1,0:T(8,128)(2,1)} collective-permute-done((bf16[96,768]{1,0:T(8,128)(2,1)}, bf16[96,768]{1,0:T(8,128)(2,1)}, u32[]{:S(2)}, u32[]{:S(2)}) %collective-permute-start.43) | collective-permute-done | bytes 147488 | tf_op jit(solution)/shard_map/ppermute | solution.py:146
  344.8 2.1 collective-permute-start.45
  346.9 2.4 multiply_subtract_fusion.1
  349.2 4.5 %collective-permute-done.46 = bf16[96,768]{1,0:T(8,128)(2,1)S(1)} collective-permute-done((bf16[96,768]{1,0:T(8,128)(2,1)S(1)}, bf16[96,768]{1,0:T(8,128)(2,1)S(1)}, u32[]{:S(2)}, u32[]{:S(2)}) %collective-permute-start.46) | collective-permute-done | bytes 147488 | tf_op jit(solution)/shard_map/ppermute | solution.py:146
  353.8 2.0 multiply_subtract_fusion
  355.8 2.1 copy.123
  364.4 5.3 %collective-permute-done.33 = bf16[1,1,2,1,96,576]{4,5,3,2,1,0:T(8,128)(2,1)} collective-permute-done((bf16[1,1,2,1,96,576]{4,5,3,2,1,0:T(8,128)(2,1)}, bf16[1,1,2,1,96,576]{4,5,3,2,1,0:T(8,128)(2,1)}, u32[]{:S(2)}, u32[]{:S(2)}) %collective-permute-start.33) | collective-permute-done | bytes 221216 | tf_op jit(solution)/shard_map/ppermute | solution.py:146
  374.6 2.1 convert_reduce_fusion.3
  377.4 3.1 collective-permute-done.49
  381.2 2.9 collective-permute-done.50
  386.2 1.6 collective-permute-done.51
  388.8 2.1 collective-permute-start.35
  392.6 2.2 collective-permute-done.55
  395.2 1.8 collective-permute-done.35
  397.1 1.6 collective-permute-done.56
  (354 shorter events, 92.8 us)
Async XLA Ops:
  1.8 43.1 %collective-permute-start.12 = (bf16[96,768]{1,0:T(8,128)(2,1)S(1)}, bf16[96,768]{1,0:T(8,128)(2,1)S(1)}, u32[]{:S(2)}, u32[]{:S(2)}) collective-permute-start(bf16[96,768]{1,0:T(8,128)(2,1)S(1)} %get-tuple-element.183), channel_id=1, source_target_pairs={{0,3},{1,2},{2,1},{3,0},{4,7},{5,6},{6,5},{7,4},{8,11},{9,10},{10,... | collective-permute-start | bytes 442376 | tf_op jit(solution)/shard_map/ppermute | solution.py:146
  6.9 38.1 %collective-permute-start.11 = (bf16[96,768]{1,0:T(8,128)(2,1)S(1)}, bf16[96,768]{1,0:T(8,128)(2,1)S(1)}, u32[]{:S(2)}, u32[]{:S(2)}) collective-permute-start(bf16[96,768]{1,0:T(8,128)(2,1)S(1)} %get-tuple-element.183), channel_id=1, source_target_pairs={{0,2},{1,3},{2,0},{3,1},{4,6},{5,7},{6,4},{7,5},{8,10},{9,11},{10,... | collective-permute-start | bytes 442376 | tf_op jit(solution)/shard_map/ppermute | solution.py:146
  6.9 39.6 %collective-permute-start.10 = (bf16[96,768]{1,0:T(8,128)(2,1)S(1)}, bf16[96,768]{1,0:T(8,128)(2,1)S(1)}, u32[]{:S(2)}, u32[]{:S(2)}) collective-permute-start(bf16[96,768]{1,0:T(8,128)(2,1)S(1)} %get-tuple-element.183), channel_id=1, source_target_pairs={{0,1},{1,0},{2,3},{3,2},{4,5},{5,4},{6,7},{7,6},{8,9},{9,8},{10,11... | collective-permute-start | bytes 442376 | tf_op jit(solution)/shard_map/ppermute | solution.py:146
  8.8 15.8 %collective-permute-start.3 = (bf16[96,576]{1,0:T(8,128)(2,1)S(1)}, bf16[96,576]{1,0:T(8,128)(2,1)S(1)}, u32[]{:S(2)}, u32[]{:S(2)}) collective-permute-start(bf16[96,576]{1,0:T(8,128)(2,1)S(1)} %copy.106), channel_id=1, source_target_pairs={{0,2},{1,3},{2,0},{3,1},{4,6},{5,7},{6,4},{7,5},{8,10},{9,11},{10,... | collective-permute-start | bytes 331784 | tf_op jit(solution)/shard_map/ppermute | solution.py:146
  11.2 16.2 %collective-permute-start = (bf16[1,1,1,1,96,576]{5,4,3,2,1,0:T(8,128)(2,1)S(1)}, bf16[1,1,1,1,96,576]{5,4,3,2,1,0:T(8,128)(2,1)S(1)}, u32[]{:S(2)}, u32[]{:S(2)}) collective-permute-start(bf16[1,1,1,1,96,576]{5,4,3,2,1,0:T(8,128)(2,1)S(1)} %bitcast.255), channel_id=1, source_target_pairs={{0,8},{4,12},{8,0},{12,4},{16,24},{20,28},{24,16},{28,20},{1,9},{5... | collective-permute-start | bytes 331784 | tf_op jit(solution)/shard_map/ppermute | solution.py:146
  24.6 22.1 %collective-permute-start.9 = (bf16[96,960]{1,0:T(8,128)(2,1)S(1)}, bf16[96,960]{1,0:T(8,128)(2,1)S(1)}, u32[]{:S(2)}, u32[]{:S(2)}) collective-permute-start(bf16[96,960]{1,0:T(8,128)(2,1)S(1)} %get-tuple-element.192), channel_id=1, source_target_pairs={{0,3},{1,2},{2,1},{3,0},{4,7},{5,6},{6,5},{7,4},{8,11},{9,10},{10,... | collective-permute-start | bytes 552968 | tf_op jit(solution)/shard_map/ppermute | solution.py:146
  27.4 5.0 %collective-permute-start.4 = (bf16[1,1,1,1,96,576]{5,4,3,2,1,0:T(8,128)(2,1)S(1)}, bf16[1,1,1,1,96,576]{5,4,3,2,1,0:T(8,128)(2,1)S(1)}, u32[]{:S(2)}, u32[]{:S(2)}) collective-permute-start(bf16[1,1,1,1,96,576]{5,4,3,2,1,0:T(8,128)(2,1)S(1)} %bitcast.264), channel_id=1, source_target_pairs={{0,16},{4,20},{8,24},{12,28},{16,0},{20,4},{24,8},{28,12},{1,17},{... | collective-permute-start | bytes 331784 | tf_op jit(solution)/shard_map/ppermute | solution.py:146
  32.4 6.2 %collective-permute-start.1 = (bf16[1,1,2,1,96,576]{5,4,3,2,1,0:T(8,128)(2,1)S(1)}, bf16[1,1,2,1,96,576]{5,4,3,2,1,0:T(8,128)(2,1)S(1)}, u32[]{:S(2)}, u32[]{:S(2)}) collective-permute-start(bf16[1,1,2,1,96,576]{5,4,3,2,1,0:T(8,128)(2,1)S(1)} %pad_maximum_fusion.10), channel_id=1, source_target_pairs={{0,16},{4,20},{8,24},{12,28},{16,0},{20,4},{24,8},{28,12},{1,17},{... | collective-permute-start | bytes 663560 | tf_op jit(solution)/shard_map/ppermute | solution.py:146
  38.6 6.2 %collective-permute-start.5 = (bf16[1,2,1,1,96,576]{5,4,3,2,1,0:T(8,128)(2,1)S(1)}, bf16[1,2,1,1,96,576]{5,4,3,2,1,0:T(8,128)(2,1)S(1)}, u32[]{:S(2)}, u32[]{:S(2)}) collective-permute-start(bf16[1,2,1,1,96,576]{5,4,3,2,1,0:T(8,128)(2,1)S(1)} %pad_maximum_fusion.11), channel_id=1, source_target_pairs={{0,8},{4,12},{8,0},{12,4},{16,24},{20,28},{24,16},{28,20},{1,9},{5... | collective-permute-start | bytes 663560 | tf_op jit(solution)/shard_map/ppermute | solution.py:146
  44.8 12.3 %collective-permute-start.2 = (bf16[1,2,2,1,96,576]{5,4,3,2,1,0:T(8,128)(2,1)S(1)}, bf16[1,2,2,1,96,576]{5,4,3,2,1,0:T(8,128)(2,1)S(1)}, u32[]{:S(2)}, u32[]{:S(2)}) collective-permute-start(bf16[1,2,2,1,96,576]{5,4,3,2,1,0:T(8,128)(2,1)S(1)} %pad_maximum_fusion.8), channel_id=1, source_target_pairs={{0,4},{4,0},{8,12},{12,8},{16,20},{20,16},{24,28},{28,24},{1,5},{5... | collective-permute-start | bytes 1327112 | tf_op jit(solution)/shard_map/ppermute | solution.py:146
  44.9 10.9 %collective-permute-start.8 = (bf16[96,960]{1,0:T(8,128)(2,1)S(1)}, bf16[96,960]{1,0:T(8,128)(2,1)S(1)}, u32[]{:S(2)}, u32[]{:S(2)}) collective-permute-start(bf16[96,960]{1,0:T(8,128)(2,1)S(1)} %get-tuple-element.192), channel_id=1, source_target_pairs={{0,2},{1,3},{2,0},{3,1},{4,6},{5,7},{6,4},{7,5},{8,10},{9,11},{10,... | collective-permute-start | bytes 552968 | tf_op jit(solution)/shard_map/ppermute | solution.py:146
  45.0 12.0 %collective-permute-start.7 = (bf16[96,960]{1,0:T(8,128)(2,1)S(1)}, bf16[96,960]{1,0:T(8,128)(2,1)S(1)}, u32[]{:S(2)}, u32[]{:S(2)}) collective-permute-start(bf16[96,960]{1,0:T(8,128)(2,1)S(1)} %get-tuple-element.192), channel_id=1, source_target_pairs={{0,1},{1,0},{2,3},{3,2},{4,5},{5,4},{6,7},{7,6},{8,9},{9,8},{10,11... | collective-permute-start | bytes 552968 | tf_op jit(solution)/shard_map/ppermute | solution.py:146
  46.5 10.7 %collective-permute-start.6 = (bf16[1,2,2,1,96,576]{5,4,3,2,1,0:T(8,128)(2,1)S(1)}, bf16[1,2,2,1,96,576]{5,4,3,2,1,0:T(8,128)(2,1)S(1)}, u32[]{:S(2)}, u32[]{:S(2)}) collective-permute-start(bf16[1,2,2,1,96,576]{5,4,3,2,1,0:T(8,128)(2,1)S(1)} %pad_maximum_fusion.9), channel_id=1, source_target_pairs={{0,4},{4,0},{8,12},{12,8},{16,20},{20,16},{24,28},{28,24},{1,5},{5... | collective-permute-start | bytes 1327112 | tf_op jit(solution)/shard_map/ppermute | solution.py:146
  46.7 26.7 %collective-permute-start.13 = (bf16[512,768]{1,0:T(8,128)(2,1)S(1)}, bf16[512,768]{1,0:T(8,128)(2,1)S(1)}, u32[]{:S(2)}, u32[]{:S(2)}) collective-permute-start(bf16[512,768]{1,0:T(8,128)(2,1)S(1)} %fusion.22), channel_id=1, source_target_pairs={{0,1},{1,0},{2,3},{3,2},{4,5},{5,4},{6,7},{7,6},{8,9},{9,8},{10,11... | collective-permute-start | bytes 2359304 | tf_op jit(solution)/shard_map/ppermute | solution.py:146
  57.8 20.3 %collective-permute-start.15 = (bf16[4,1,1,1,96,768]{5,4,0,3,2,1:T(8,128)(2,1)S(1)}, bf16[4,1,1,1,96,768]{5,4,0,3,2,1:T(8,128)(2,1)S(1)}, u32[]{:S(2)}, u32[]{:S(2)}) collective-permute-start(bf16[4,1,1,1,96,768]{5,4,0,3,2,1:T(8,128)(2,1)S(1)} %maximum_bitcast_fusion.4), channel_id=1, source_target_pairs={{0,16},{4,20},{8,24},{12,28},{16,0},{20,4},{24,8},{28,12},{1,17},{... | collective-permute-start | bytes 1769480 | tf_op jit(solution)/shard_map/ppermute | solution.py:146
  74.0 19.2 %collective-permute-start.14 = (bf16[4,1,1,1,96,960]{5,4,0,3,2,1:T(8,128)(2,1)S(1)}, bf16[4,1,1,1,96,960]{5,4,0,3,2,1:T(8,128)(2,1)S(1)}, u32[]{:S(2)}, u32[]{:S(2)}) collective-permute-start(bf16[4,1,1,1,96,960]{5,4,0,3,2,1:T(8,128)(2,1)S(1)} %maximum_bitcast_fusion.3), channel_id=1, source_target_pairs={{0,8},{4,12},{8,0},{12,4},{16,24},{20,28},{24,16},{28,20},{1,9},{5... | collective-permute-start | bytes 2211848 | tf_op jit(solution)/shard_map/ppermute | solution.py:146
  93.5 26.8 %collective-permute-start.17 = (bf16[4,2,1,1,96,768]{5,4,0,3,2,1:T(8,128)(2,1)S(1)}, bf16[4,2,1,1,96,768]{5,4,0,3,2,1:T(8,128)(2,1)S(1)}, u32[]{:S(2)}, u32[]{:S(2)}) collective-permute-start(bf16[4,2,1,1,96,768]{5,4,0,3,2,1:T(8,128)(2,1)S(1)} %pad_maximum_fusion.5), channel_id=1, source_target_pairs={{0,8},{4,12},{8,0},{12,4},{16,24},{20,28},{24,16},{28,20},{1,9},{5... | collective-permute-start | bytes 3538952 | tf_op jit(solution)/shard_map/ppermute | solution.py:146
  95.1 34.9 %collective-permute-start.16 = (bf16[4,1,2,1,96,960]{5,4,0,3,2,1:T(8,128)(2,1)S(1)}, bf16[4,1,2,1,96,960]{5,4,0,3,2,1:T(8,128)(2,1)S(1)}, u32[]{:S(2)}, u32[]{:S(2)}) collective-permute-start(bf16[4,1,2,1,96,960]{5,4,0,3,2,1:T(8,128)(2,1)S(1)} %pad_maximum_fusion.4), channel_id=1, source_target_pairs={{0,16},{4,20},{8,24},{12,28},{16,0},{20,4},{24,8},{28,12},{1,17},{... | collective-permute-start | bytes 4423688 | tf_op jit(solution)/shard_map/ppermute | solution.py:146
  132.1 13.8 %collective-permute-start.20 = (bf16[4,2,2,1,96,768]{5,4,0,3,2,1:T(8,128)(2,1)}, bf16[4,2,2,1,96,768]{5,4,0,3,2,1:T(8,128)(2,1)}, u32[]{:S(2)}, u32[]{:S(2)}) collective-permute-start(bf16[4,2,2,1,96,768]{5,4,0,3,2,1:T(8,128)(2,1)} %pad_maximum_fusion.3), channel_id=1, source_target_pairs={{0,4},{4,0},{8,12},{12,8},{16,20},{20,16},{24,28},{28,24},{1,5},{5... | collective-permute-start | bytes 7077896 | tf_op jit(solution)/shard_map/ppermute | solution.py:146
  132.1 19.8 %collective-permute-start.19 = (bf16[4,2,2,1,96,960]{5,4,0,3,2,1:T(8,128)(2,1)}, bf16[4,2,2,1,96,960]{5,4,0,3,2,1:T(8,128)(2,1)}, u32[]{:S(2)}, u32[]{:S(2)}) collective-permute-start(bf16[4,2,2,1,96,960]{5,4,0,3,2,1:T(8,128)(2,1)} %pad_maximum_fusion.2), channel_id=1, source_target_pairs={{0,4},{4,0},{8,12},{12,8},{16,20},{20,16},{24,28},{28,24},{1,5},{5... | collective-permute-start | bytes 8847368 | tf_op jit(solution)/shard_map/ppermute | solution.py:146
  133.6 11.2 %collective-permute-start.18 = (bf16[2,192,512]{2,1,0:T(8,128)(2,1)}, bf16[2,192,512]{2,1,0:T(8,128)(2,1)S(1)}, u32[]{:S(2)}, u32[]{:S(2)}) collective-permute-start(bf16[2,192,512]{2,1,0:T(8,128)(2,1)} %get-tuple-element.171), channel_id=1, source_target_pairs={{0,1},{1,0},{2,3},{3,2},{4,5},{5,4},{6,7},{7,6},{8,9},{9,8},{10,11... | collective-permute-start | bytes 1179656 | tf_op jit(solution)/shard_map/ppermute | solution.py:146
  134.3 31.8 %copy-start.53 = (f32[4,768]{1,0:T(4,128)}, f32[4,768]{1,0:T(4,128)S(1)}, u32[]{:S(2)}) copy-start(f32[4,768]{1,0:T(4,128)S(1)} %pad_maximum_fusion.14) | copy-start | bytes 36868
  186.5 27.6 %collective-permute-start.21 = (bf16[4,2,2,1,96,768]{5,4,3,2,1,0:T(8,128)(2,1)}, bf16[4,2,2,1,96,768]{5,4,3,2,1,0:T(8,128)(2,1)}, u32[]{:S(2)}, u32[]{:S(2)}) collective-permute-start(bf16[4,2,2,1,96,768]{5,4,3,2,1,0:T(8,128)(2,1)} %constant_dynamic-slice_fusion.18), channel_id=1, source_target_pairs={{0,4},{4,0},{8,12},{12,8},{16,20},{20,16},{24,28},{28,24},{1,5},{5... | collective-permute-start | bytes 7077896 | tf_op jit(solution)/shard_map/ppermute | solution.py:146
  193.2 24.9 %collective-permute-start.22 = (bf16[4,2,2,1,96,768]{5,4,3,2,1,0:T(8,128)(2,1)}, bf16[4,2,2,1,96,768]{5,4,3,2,1,0:T(8,128)(2,1)}, u32[]{:S(2)}, u32[]{:S(2)}) collective-permute-start(bf16[4,2,2,1,96,768]{5,4,3,2,1,0:T(8,128)(2,1)} %constant_dynamic-slice_fusion.17), channel_id=1, source_target_pairs={{0,4},{4,0},{8,12},{12,8},{16,20},{20,16},{24,28},{28,24},{1,5},{5... | collective-permute-start | bytes 7077896 | tf_op jit(solution)/shard_map/ppermute | solution.py:146
  228.7 9.4 %collective-permute-start.36 = (bf16[4,2,2,1,96,192]{4,5,3,2,1,0:T(8,128)(2,1)}, bf16[4,2,2,1,96,192]{4,5,3,2,1,0:T(8,128)(2,1)}, u32[]{:S(2)}, u32[]{:S(2)}) collective-permute-start(bf16[4,2,2,1,96,192]{4,5,3,2,1,0:T(8,128)(2,1)} %copy.147), channel_id=1, source_target_pairs={{0,4},{4,0},{8,12},{12,8},{16,20},{20,16},{24,28},{28,24},{1,5},{5... | collective-permute-start | bytes 1769480 | tf_op jit(solution)/shard_map/ppermute | solution.py:146
  233.4 39.8 %collective-permute-start.23 = (bf16[2,192,512]{2,1,0:T(8,128)(2,1)}, bf16[2,192,512]{2,1,0:T(8,128)(2,1)}, u32[]{:S(2)}, u32[]{:S(2)}) collective-permute-start(bf16[2,192,512]{2,1,0:T(8,128)(2,1)} %slice_bitcast_fusion), channel_id=1, source_target_pairs={{0,1},{1,0},{2,3},{3,2},{4,5},{5,4},{6,7},{7,6},{8,9},{9,8},{10,11... | collective-permute-start | bytes 1179656 | tf_op jit(solution)/shard_map/ppermute | solution.py:146
  235.2 46.7 %collective-permute-start.24 = (bf16[4,2,1,1,96,768]{5,4,3,2,1,0:T(8,128)(2,1)}, bf16[4,2,1,1,96,768]{5,4,3,2,1,0:T(8,128)(2,1)}, u32[]{:S(2)}, u32[]{:S(2)}) collective-permute-start(bf16[4,2,1,1,96,768]{5,4,3,2,1,0:T(8,128)(2,1)} %constant_dynamic-slice_fusion.16), channel_id=1, source_target_pairs={{0,8},{4,12},{8,0},{12,4},{16,24},{20,28},{24,16},{28,20},{1,9},{5... | collective-permute-start | bytes 3538952 | tf_op jit(solution)/shard_map/ppermute | solution.py:146
  239.9 33.3 %copy-start.29 = (bf16[4,192,512]{2,1,0:T(8,128)(2,1)S(1)}, bf16[4,192,512]{2,1,0:T(8,128)(2,1)}, u32[]{:S(2)}) copy-start(bf16[4,192,512]{2,1,0:T(8,128)(2,1)} %copy-done.28) | copy-start | bytes 2359300
  239.9 31.5 %collective-permute-start.37 = (bf16[4,2,1,1,96,192]{4,5,3,2,1,0:T(8,128)(2,1)S(1)}, bf16[4,2,1,1,96,192]{4,5,3,2,1,0:T(8,128)(2,1)S(1)}, u32[]{:S(2)}, u32[]{:S(2)}) collective-permute-start(bf16[4,2,1,1,96,192]{4,5,3,2,1,0:T(8,128)(2,1)S(1)} %constant_dynamic-slice_fusion.1), channel_id=1, source_target_pairs={{0,8},{4,12},{8,0},{12,4},{16,24},{20,28},{24,16},{28,20},{1,9},{5... | collective-permute-start | bytes 884744 | tf_op jit(solution)/shard_map/ppermute | solution.py:146
  241.5 42.1 %collective-permute-start.25 = (bf16[4,1,2,1,96,768]{5,4,3,2,1,0:T(8,128)(2,1)S(1)}, bf16[4,1,2,1,96,768]{5,4,3,2,1,0:T(8,128)(2,1)S(1)}, u32[]{:S(2)}, u32[]{:S(2)}) collective-permute-start(bf16[4,1,2,1,96,768]{5,4,3,2,1,0:T(8,128)(2,1)S(1)} %constant_dynamic-slice_fusion.15), channel_id=1, source_target_pairs={{0,16},{4,20},{8,24},{12,28},{16,0},{20,4},{24,8},{28,12},{1,17},{... | collective-permute-start | bytes 3538952 | tf_op jit(solution)/shard_map/ppermute | solution.py:146
  243.1 31.2 %copy-start.50 = (f32[6144]{0:T(1024)}, f32[6144]{0:T(1024)S(1)}, u32[]{:S(2)}) copy-start(f32[6144]{0:T(1024)S(1)} %constant_dynamic-update-slice_fusion.3) | copy-start | bytes 73732
  271.6 5.7 %collective-permute-start.38 = (bf16[4,1,1,1,96,192]{4,5,3,2,1,0:T(8,128)(2,1)S(1)}, bf16[4,1,1,1,96,192]{4,5,3,2,1,0:T(8,128)(2,1)S(1)}, u32[]{:S(2)}, u32[]{:S(2)}) collective-permute-start(bf16[4,1,1,1,96,192]{4,5,3,2,1,0:T(8,128)(2,1)S(1)} %constant_dynamic-slice_fusion), channel_id=1, source_target_pairs={{0,16},{4,20},{8,24},{12,28},{16,0},{20,4},{24,8},{28,12},{1,17},{... | collective-permute-start | bytes 442376 | tf_op jit(solution)/shard_map/ppermute | solution.py:146
  277.4 8.2 %collective-permute-start.41 = (bf16[96,192]{0,1:T(8,128)(2,1)S(1)}, bf16[96,192]{0,1:T(8,128)(2,1)S(1)}, u32[]{:S(2)}, u32[]{:S(2)}) collective-permute-start(bf16[96,192]{0,1:T(8,128)(2,1)S(1)} %get-tuple-element.189), channel_id=1, source_target_pairs={{0,3},{1,2},{2,1},{3,0},{4,7},{5,6},{6,5},{7,4},{8,11},{9,10},{10,... | collective-permute-start | bytes 110600 | tf_op jit(solution)/shard_map/ppermute | solution.py:146
  279.0 6.6 %collective-permute-start.40 = (bf16[96,192]{0,1:T(8,128)(2,1)S(1)}, bf16[96,192]{0,1:T(8,128)(2,1)S(1)}, u32[]{:S(2)}, u32[]{:S(2)}) collective-permute-start(bf16[96,192]{0,1:T(8,128)(2,1)S(1)} %get-tuple-element.190), channel_id=1, source_target_pairs={{0,2},{1,3},{2,0},{3,1},{4,6},{5,7},{6,4},{7,5},{8,10},{9,11},{10,... | collective-permute-start | bytes 110600 | tf_op jit(solution)/shard_map/ppermute | solution.py:146
  280.3 5.4 %collective-permute-start.39 = (bf16[96,192]{0,1:T(8,128)(2,1)S(1)}, bf16[96,192]{0,1:T(8,128)(2,1)S(1)}, u32[]{:S(2)}, u32[]{:S(2)}) collective-permute-start(bf16[96,192]{0,1:T(8,128)(2,1)S(1)} %get-tuple-element.188), channel_id=1, source_target_pairs={{0,1},{1,0},{2,3},{3,2},{4,5},{5,4},{6,7},{7,6},{8,9},{9,8},{10,11... | collective-permute-start | bytes 110600 | tf_op jit(solution)/shard_map/ppermute | solution.py:146
  284.1 19.5 %collective-permute-start.26 = (bf16[4,1,1,1,96,768]{5,4,3,2,1,0:T(8,128)(2,1)S(1)}, bf16[4,1,1,1,96,768]{5,4,3,2,1,0:T(8,128)(2,1)S(1)}, u32[]{:S(2)}, u32[]{:S(2)}) collective-permute-start(bf16[4,1,1,1,96,768]{5,4,3,2,1,0:T(8,128)(2,1)S(1)} %constant_dynamic-slice_fusion.14), channel_id=1, source_target_pairs={{0,16},{4,20},{8,24},{12,28},{16,0},{20,4},{24,8},{28,12},{1,17},{... | collective-permute-start | bytes 1769480 | tf_op jit(solution)/shard_map/ppermute | solution.py:146
  286.5 18.1 %collective-permute-start.27 = (bf16[4,1,1,1,96,768]{5,4,3,2,1,0:T(8,128)(2,1)S(1)}, bf16[4,1,1,1,96,768]{5,4,3,2,1,0:T(8,128)(2,1)S(1)}, u32[]{:S(2)}, u32[]{:S(2)}) collective-permute-start(bf16[4,1,1,1,96,768]{5,4,3,2,1,0:T(8,128)(2,1)S(1)} %constant_dynamic-slice_fusion.13), channel_id=1, source_target_pairs={{0,8},{4,12},{8,0},{12,4},{16,24},{20,28},{24,16},{28,20},{1,9},{5... | collective-permute-start | bytes 1769480 | tf_op jit(solution)/shard_map/ppermute | solution.py:146
  313.1 59.3 %collective-permute-start.28 = (bf16[512,768]{1,0:T(8,128)(2,1)}, bf16[512,768]{1,0:T(8,128)(2,1)S(1)}, u32[]{:S(2)}, u32[]{:S(2)}) collective-permute-start(bf16[512,768]{1,0:T(8,128)(2,1)} %constant_dynamic-slice_fusion.12), channel_id=1, source_target_pairs={{0,1},{1,0},{2,3},{3,2},{4,5},{5,4},{6,7},{7,6},{8,9},{9,8},{10,11... | collective-permute-start | bytes 2359304 | tf_op jit(solution)/shard_map/ppermute | solution.py:146
  318.5 37.3 %collective-permute-start.32 = (bf16[1,2,2,1,96,576]{5,4,3,2,1,0:T(8,128)(2,1)}, bf16[1,2,2,1,96,576]{5,4,3,2,1,0:T(8,128)(2,1)}, u32[]{:S(2)}, u32[]{:S(2)}) collective-permute-start(bf16[1,2,2,1,96,576]{5,4,3,2,1,0:T(8,128)(2,1)} %get-tuple-element.165), channel_id=1, source_target_pairs={{0,4},{4,0},{8,12},{12,8},{16,20},{20,16},{24,28},{28,24},{1,5},{5... | collective-permute-start | bytes 1327112 | tf_op jit(solution)/shard_map/ppermute | solution.py:146
  321.0 25.9 %copy-start.20 = (f32[96,768]{1,0:T(8,128)S(1)}, f32[96,768]{1,0:T(8,128)}, u32[]{:S(2)}) copy-start(f32[96,768]{1,0:T(8,128)} %param.21) | copy-start | bytes 884740
  321.0 25.9 %copy-start.39 = (f32[96,768]{1,0:T(8,128)S(1)}, f32[96,768]{1,0:T(8,128)}, u32[]{:S(2)}) copy-start(f32[96,768]{1,0:T(8,128)} %param.29) | copy-start | bytes 884740
  324.2 8.9 %collective-permute-start.44 = (bf16[96,768]{1,0:T(8,128)(2,1)}, bf16[96,768]{1,0:T(8,128)(2,1)}, u32[]{:S(2)}, u32[]{:S(2)}) collective-permute-start(bf16[96,768]{1,0:T(8,128)(2,1)} %get-tuple-element.176), channel_id=1, source_target_pairs={{0,3},{1,2},{2,1},{3,0},{4,7},{5,6},{6,5},{7,4},{8,11},{9,10},{10,... | collective-permute-start | bytes 442376 | tf_op jit(solution)/shard_map/ppermute | solution.py:146
  326.1 18.7 %collective-permute-start.43 = (bf16[96,768]{1,0:T(8,128)(2,1)}, bf16[96,768]{1,0:T(8,128)(2,1)}, u32[]{:S(2)}, u32[]{:S(2)}) collective-permute-start(bf16[96,768]{1,0:T(8,128)(2,1)} %get-tuple-element.177), channel_id=1, source_target_pairs={{0,2},{1,3},{2,0},{3,1},{4,6},{5,7},{6,4},{7,5},{8,10},{9,11},{10,... | collective-permute-start | bytes 442376 | tf_op jit(solution)/shard_map/ppermute | solution.py:146
  327.2 17.6 %collective-permute-start.42 = (bf16[96,768]{1,0:T(8,128)(2,1)}, bf16[96,768]{1,0:T(8,128)(2,1)}, u32[]{:S(2)}, u32[]{:S(2)}) collective-permute-start(bf16[96,768]{1,0:T(8,128)(2,1)} %get-tuple-element.175), channel_id=1, source_target_pairs={{0,1},{1,0},{2,3},{3,2},{4,5},{5,4},{6,7},{7,6},{8,9},{9,8},{10,11... | collective-permute-start | bytes 442376 | tf_op jit(solution)/shard_map/ppermute | solution.py:146
  329.7 24.1 %copy-start.21 = (f32[768,96]{0,1:T(8,128)S(1)}, f32[768,96]{0,1:T(8,128)}, u32[]{:S(2)}) copy-start(f32[768,96]{0,1:T(8,128)} %param.22) | copy-start | bytes 884740
  333.1 16.1 %collective-permute-start.47 = (bf16[96,768]{1,0:T(8,128)(2,1)S(1)}, bf16[96,768]{1,0:T(8,128)(2,1)S(1)}, u32[]{:S(2)}, u32[]{:S(2)}) collective-permute-start(bf16[96,768]{1,0:T(8,128)(2,1)S(1)} %get-tuple-element.173), channel_id=1, source_target_pairs={{0,3},{1,2},{2,1},{3,0},{4,7},{5,6},{6,5},{7,4},{8,11},{9,10},{10,... | collective-permute-start | bytes 442376 | tf_op jit(solution)/shard_map/ppermute | solution.py:146
  344.8 9.0 %collective-permute-start.46 = (bf16[96,768]{1,0:T(8,128)(2,1)S(1)}, bf16[96,768]{1,0:T(8,128)(2,1)S(1)}, u32[]{:S(2)}, u32[]{:S(2)}) collective-permute-start(bf16[96,768]{1,0:T(8,128)(2,1)S(1)} %get-tuple-element.174), channel_id=1, source_target_pairs={{0,2},{1,3},{2,0},{3,1},{4,6},{5,7},{6,4},{7,5},{8,10},{9,11},{10,... | collective-permute-start | bytes 442376 | tf_op jit(solution)/shard_map/ppermute | solution.py:146
  344.8 9.0 %collective-permute-start.45 = (bf16[96,768]{1,0:T(8,128)(2,1)S(1)}, bf16[96,768]{1,0:T(8,128)(2,1)S(1)}, u32[]{:S(2)}, u32[]{:S(2)}) collective-permute-start(bf16[96,768]{1,0:T(8,128)(2,1)S(1)} %get-tuple-element.172), channel_id=1, source_target_pairs={{0,1},{1,0},{2,3},{3,2},{4,5},{5,4},{6,7},{7,6},{8,9},{9,8},{10,11... | collective-permute-start | bytes 442376 | tf_op jit(solution)/shard_map/ppermute | solution.py:146
  349.2 12.0 %collective-permute-start.29 = (bf16[1,2,2,1,96,576]{5,4,3,2,1,0:T(8,128)(2,1)}, bf16[1,2,2,1,96,576]{5,4,3,2,1,0:T(8,128)(2,1)}, u32[]{:S(2)}, u32[]{:S(2)}) collective-permute-start(bf16[1,2,2,1,96,576]{5,4,3,2,1,0:T(8,128)(2,1)} %get-tuple-element.163), channel_id=1, source_target_pairs={{0,4},{4,0},{8,12},{12,8},{16,20},{20,16},{24,28},{28,24},{1,5},{5... | collective-permute-start | bytes 1327112 | tf_op jit(solution)/shard_map/ppermute | solution.py:146
  360.7 9.0 %collective-permute-start.33 = (bf16[1,1,2,1,96,576]{4,5,3,2,1,0:T(8,128)(2,1)}, bf16[1,1,2,1,96,576]{4,5,3,2,1,0:T(8,128)(2,1)}, u32[]{:S(2)}, u32[]{:S(2)}) collective-permute-start(bf16[1,1,2,1,96,576]{4,5,3,2,1,0:T(8,128)(2,1)} %constant_dynamic-slice_fusion.5), channel_id=1, source_target_pairs={{0,16},{4,20},{8,24},{12,28},{16,0},{20,4},{24,8},{28,12},{1,17},{... | collective-permute-start | bytes 663560 | tf_op jit(solution)/shard_map/ppermute | solution.py:146
  362.8 9.5 %collective-permute-start.30 = (bf16[1,2,1,1,96,576]{4,5,3,2,1,0:T(8,128)(2,1)S(1)}, bf16[1,2,1,1,96,576]{4,5,3,2,1,0:T(8,128)(2,1)S(1)}, u32[]{:S(2)}, u32[]{:S(2)}) collective-permute-start(bf16[1,2,1,1,96,576]{4,5,3,2,1,0:T(8,128)(2,1)S(1)} %constant_dynamic-slice_fusion.9), channel_id=1, source_target_pairs={{0,8},{4,12},{8,0},{12,4},{16,24},{20,28},{24,16},{28,20},{1,9},{5... | collective-permute-start | bytes 663560 | tf_op jit(solution)/shard_map/ppermute | solution.py:146
  370.8 18.0 %collective-permute-start.34 = (bf16[1,1,1,1,96,576]{4,5,3,2,1,0:T(8,128)(2,1)S(1)}, bf16[1,1,1,1,96,576]{4,5,3,2,1,0:T(8,128)(2,1)S(1)}, u32[]{:S(2)}, u32[]{:S(2)}) collective-permute-start(bf16[1,1,1,1,96,576]{4,5,3,2,1,0:T(8,128)(2,1)S(1)} %constant_dynamic-slice_fusion.4), channel_id=1, source_target_pairs={{0,8},{4,12},{8,0},{12,4},{16,24},{20,28},{24,16},{28,20},{1,9},{5... | collective-permute-start | bytes 331784 | tf_op jit(solution)/shard_map/ppermute | solution.py:146
  374.1 2.6 collective-permute-start.48
  376.7 3.8 collective-permute-start.49
  380.5 3.7 collective-permute-start.50
  381.2 3.8 collective-permute-start.53
  384.2 3.7 collective-permute-start.51
  384.2 11.0 %collective-permute-start.31 = (bf16[1,1,1,1,96,576]{4,5,3,2,1,0:T(8,128)(2,1)S(1)}, bf16[1,1,1,1,96,576]{4,5,3,2,1,0:T(8,128)(2,1)S(1)}, u32[]{:S(2)}, u32[]{:S(2)}) collective-permute-start(bf16[1,1,1,1,96,576]{4,5,3,2,1,0:T(8,128)(2,1)S(1)} %constant_dynamic-slice_fusion.8), channel_id=1, source_target_pairs={{0,16},{4,20},{8,24},{12,28},{16,0},{20,4},{24,8},{28,12},{1,17},{... | collective-permute-start | bytes 331784 | tf_op jit(solution)/shard_map/ppermute | solution.py:146
  385.0 5.9 %collective-permute-start.54 = (f32[6144]{0:T(1024)S(1)}, f32[6144]{0:T(1024)S(1)}, u32[]{:S(2)}, u32[]{:S(2)}) collective-permute-start(f32[6144]{0:T(1024)S(1)} %add.528), channel_id=1, source_target_pairs={{0,8},{4,12},{8,0},{12,4},{16,24},{20,28},{24,16},{28,20},{1,9},{5... | collective-permute-start | bytes 73736 | tf_op jit(solution)/shard_map/ppermute | solution.py:146
  387.9 4.7 %collective-permute-start.52 = (f32[3072]{0:T(1024)S(1)}, f32[3072]{0:T(1024)S(1)}, u32[]{:S(2)}, u32[]{:S(2)}) collective-permute-start(f32[3072]{0:T(1024)S(1)} %add.522), channel_id=1, source_target_pairs={{0,2},{1,3},{2,0},{3,1},{4,6},{5,7},{6,4},{7,5},{8,10},{9,11},{10,... | collective-permute-start | bytes 36872 | tf_op jit(solution)/shard_map/ppermute | solution.py:146
  388.8 8.2 %collective-permute-start.35 = (bf16[96,576]{0,1:T(8,128)(2,1)S(1)}, bf16[96,576]{0,1:T(8,128)(2,1)S(1)}, u32[]{:S(2)}, u32[]{:S(2)}) collective-permute-start(bf16[96,576]{0,1:T(8,128)(2,1)S(1)} %fusion.52), channel_id=1, source_target_pairs={{0,2},{1,3},{2,0},{3,1},{4,6},{5,7},{6,4},{7,5},{8,10},{9,11},{10,... | collective-permute-start | bytes 331784 | tf_op jit(solution)/shard_map/ppermute | solution.py:146
  390.9 3.9 collective-permute-start.55
  394.8 3.8 collective-permute-start.56
  398.7 4.8 %collective-permute-start.57 = (f32[6144]{0:T(1024)S(1)}, f32[6144]{0:T(1024)S(1)}, u32[]{:S(2)}, u32[]{:S(2)}) collective-permute-start(f32[6144]{0:T(1024)S(1)} %add.531), channel_id=1, source_target_pairs={{0,2},{1,3},{2,0},{3,1},{4,6},{5,7},{6,4},{7,5},{8,10},{9,11},{10,... | collective-permute-start | bytes 73736 | tf_op jit(solution)/shard_map/ppermute | solution.py:146
  (59 other events, 420.9 us)
